TPU v7x, 256 devices: a whole 4x4x8 slice. The times are simulated.
256 devices in a mesh: row: 32 (over x, y, core), col: 8 (over z).
Axes of the slice: x: 4, y: 4, z: 8, core: 2. Of those that a mesh axis runs over, the one named last changes fastest.
Arguments:
- stored: float32 [16384, 4, 4096], P('row', None, 'col'), may hold values from -6 to 6
- panel: float32 [16384, 256], P('row', 'col'), may hold values from -620 to 620, as said below
Outputs:
- updated: float32 [16384, 4, 4096], P('row', None, 'col')
Inputs may be any that keep to these rules, and one draw needn't show every extreme that they name: The panel has full column rank.
All inputs are finite; a program needn't handle non-finite values.
Results may differ from a plain program's by a relative error of at most 0.00007.
Values sent between devices are 32-bit elements; how exact they have to be, the bound alone decides.
A program may use at most 64 MiB of HBM per device.

v0:
```python
import jax
import jax.numpy as jnp
from jax import lax
from jax.sharding import PartitionSpec as P


def from_root(block, axis, owner):
    block = jnp.where(lax.axis_index(axis) == owner, block, jnp.zeros_like(block))
    return lax.psum(block, axis)


def to_columns(rowform, tile_cols):
    col_count = lax.axis_size("col")
    col_index = lax.axis_index("col")
    received = [
        from_root(rowform, "row", slot * col_count + col_index) for slot in range(tile_cols)
    ]
    return jnp.stack(received, 0)


def body(stored, panel):
    highest = lax.Precision.HIGHEST
    tile = stored.shape[0]
    tile_cols = stored.shape[1]
    row_index = lax.axis_index("row")
    col_index = lax.axis_index("col")
    col_count = lax.axis_size("col")
    rows_panel = lax.all_gather(panel, "col", axis=1, tiled=True)
    gram = jnp.dot(rows_panel.T, rows_panel, precision=highest)
    gram = lax.psum(gram, "row")
    factor = jnp.linalg.cholesky(gram)
    basis = lax.linalg.triangular_solve(
        factor, rows_panel, left_side=False, lower=True, transpose_a=True
    )
    basis_cols = to_columns(basis, tile_cols)
    global_cols = jnp.arange(tile_cols, dtype=jnp.int32) * col_count + col_index
    below = (global_cols < row_index)[None, :, None]
    on_diag = (global_cols == row_index)[None, :, None]
    inner_row = jnp.arange(tile, dtype=jnp.int32)[:, None, None]
    inner_col = jnp.arange(tile, dtype=jnp.int32)[None, None, :]
    lower_part = jnp.where(below | on_diag & (inner_row >= inner_col), stored, 0.0)
    strict_diag = jnp.where(on_diag & (inner_row > inner_col), stored, 0.0)
    mirrored = jnp.where(below, stored, 0.0) + strict_diag
    row_terms = jnp.einsum("ikj,kjn->in", lower_part, basis_cols, precision=highest)
    col_terms = jnp.einsum("ikj,in->kjn", mirrored, basis, precision=highest)
    coupling_part = jnp.einsum("in,im->nm", basis, row_terms, precision=highest)
    coupling_part = coupling_part + jnp.einsum(
        "kjn,kjm->nm", basis_cols, col_terms, precision=highest
    )
    col_sums, coupling_rows = lax.psum((col_terms, coupling_part), "row")
    owner_slot = row_index // col_count
    own_block = lax.dynamic_index_in_dim(col_sums, owner_slot, 0, keepdims=False)
    owned = row_index % col_count == col_index
    row_terms = row_terms + jnp.where(owned, own_block, 0.0)
    product, coupling = lax.psum((row_terms, coupling_rows), "col")
    correction = 2.0 * product - 2.0 * jnp.dot(basis, coupling, precision=highest)
    correction_cols = to_columns(correction, tile_cols)
    left_pair = jnp.concatenate([basis, correction], 1)
    right_pair = jnp.concatenate([correction_cols, basis_cols], 2)
    update = jnp.einsum("in,kjn->ikj", left_pair, right_pair, precision=highest)
    whole_tiles = lower_part + jnp.swapaxes(strict_diag, 0, 2)
    return jnp.where(below | on_diag, whole_tiles - update, 0.0)


def solution(mesh):
    in_specs = (P("row", None, "col"), P("row", "col"))
    out_specs = P("row", None, "col")
    return jax.shard_map(body, mesh=mesh, in_specs=in_specs, out_specs=out_specs, check_vma=False)
```

profile of v0, /device:TPU:7, one launch (start us, length us, event | category | flops | bytes accessed | tf_op | source)
XLA Modules:
  0.0 680.9 jit_solution(10254798525036615442)
XLA Ops:
  6.5 0.0 all-reduce.11.cloned.1.call-start
  6.5 23.1 %all_gather.3 = f32[512,256]{0,1:T(8,128)S(1)} all-gather(f32[512,32]{0,1:T(8,128)} %param.3), channel_id=1, replica_groups=mesh['row'=32,'col'=8] {'col'}, dimensions={1}, use_global_device_ids=true | all-gather | bytes 589824 | tf_op jit(solution)/shard_map/all_gather | solution.py:28
  29.6 1.3 fusion.47
  31.0 0.0 all-reduce.11.cloned.1.call-update
  31.0 0.0 all-reduce.17.cloned.1.call-start
  31.1 115.6 %all-reduce.11.cloned.1.call-done = f32[256,256]{0,1:T(8,128)} async-done(((f32[256,256]{0,1:T(8,128)}), f32[256,256]{0,1:T(8,128)}) %all-reduce.11.cloned.1.call-update) | async-done | bytes 262160 | tf_op jit(solution)/shard_map/psum | solution.py:30
  146.7 1.1 copy.8
  147.8 1.0 fusion.32
  148.8 11.7 %cholesky.50 = f32[128,128]{1,0:T(8,128)S(1)} custom-call(f32[128,128]{1,0:T(8,128)S(1)} %cholesky.118), custom_call_target="Cholesky" | custom-call | tf_op jit(solution)/shard_map/jit(cholesky)/cholesky | solution.py:31
  160.5 9.8 %custom-call.14 = f32[1,128,128]{1,2,0:T(8,128)S(1)} custom-call(f32[1,128,128]{2,1,0:T(8,128)S(1)} %get-tuple-element.49), custom_call_target="InvertDiagBlocksLowerTriangular" | custom-call | tf_op jit(solution)/shard_map/jit(cholesky)/cholesky | solution.py:31
  170.4 0.2 constant_dynamic-update-slice_fusion.4
  170.6 0.3 convolution_subtract_fusion.1
  170.9 11.7 %cholesky.105 = f32[128,128]{1,0:T(8,128)S(1)} custom-call(f32[128,128]{1,0:T(8,128)S(1)} %convolution_subtract_fusion.1), custom_call_target="Cholesky" | custom-call | tf_op jit(solution)/shard_map/jit(cholesky)/cholesky | solution.py:31
  182.6 0.7 compare_reduce_fusion
  184.6 0.1 triangular_solve.59
  184.7 4.4 while.1
  185.2 0.6 fusion.60
  185.7 1.4 bitcast_dynamic-update-slice_fusion.2
  187.1 0.6 fusion.60
  187.7 1.4 bitcast_dynamic-update-slice_fusion.2
  189.1 19.7 %custom-call.15 = f32[2,128,128]{1,2,0:T(8,128)S(1)} custom-call(f32[2,128,128]{2,1,0:T(8,128)S(1)} %get-tuple-element.12), custom_call_target="InvertDiagBlocksLowerTriangular" | custom-call | tf_op jit(solution)/shard_map/triangular_solve | solution.py:32
  208.8 0.4 fusion.30
  209.2 0.4 convolution_subtract_fusion
  209.6 0.4 fusion.33
  210.1 0.7 copy-done.3
  210.8 1.4 select_bitcast_fusion.4
  212.2 0.0 all-reduce.17.cloned.1.call-update
  212.2 0.0 all-reduce.15.cloned.1.call-start
  212.3 0.1 iota_compare_fusion
  212.3 0.5 broadcast_and_fusion
  212.9 1.2 copy.5
  214.1 5.2 copy.3
  219.3 0.8 iota_compare_fusion.1
  220.1 9.9 %fusion.10 = f32[4,512,256]{2,1,0:T(8,128)S(1)} fusion(f32[512,4,512]{2,1,0:T(4,128)} %param.2, pred[512,4,512]{2,0,1:T(32,128)(4,1)S(1)} %copy.5, pred[4]{0:T(512)(128)(4,1)S(1)} %get-tuple-element.34, f32[512,128]{0,1:T(8,128)} %copy-done.3, f32[512,128]{0,1:T(8,128)S(1)} %bitcast.70), kind=kOutput, calls=%fused_computation.14 | convolution fusion | flops 3224502272 | bytes 7864324 | tf_op jit(solution)/shard_map/ikj,in->kjn/dot_general | solution.py:45
  230.0 2.0 copy.15
  232.0 98.0 %all-reduce.17.cloned.1.call-done = (f32[1,512,256]{1,2,0:T(8,128)}, f32[1,512,256]{1,2,0:T(8,128)}, f32[1,512,256]{1,2,0:T(8,128)}, f32[1,512,256]{1,2,0:T(8,128)}) async-done(((f32[1,512,256]{1,2,0:T(8,128)}, f32[1,512,256]{1,2,0:T(8,128)}, f32[1,512,256]{1,2,0:T(8,128)}, f32[1,512,256]{1,2,0:T(8,128)}), (f32[1,512,256]{1,2,0:T(8,128)}, f32[1,512,256]{1,2,0:T(8,128)}, f32[1,512,256]{1,2,0:T(8,128)}, ...) | async-done | bytes 2097168 | tf_op jit(solution)/shard_map/psum | solution.py:9
  330.0 1.2 constant_dynamic-update-slice_fusion.3
  331.2 1.3 constant_dynamic-update-slice_fusion.2
  332.5 1.1 constant_dynamic-update-slice_fusion.1
  333.6 1.1 constant_dynamic-update-slice_fusion
  334.7 0.0 copy-start.1
  334.7 1.9 convolution_bitcast_fusion
  336.6 0.0 copy-done
  336.6 0.0 copy-done.5
  336.6 0.0 copy-start.4
  336.7 7.1 %fusion.23 = f32[512,256]{1,0:T(8,128)S(1)} fusion(f32[4,512,256]{1,2,0:T(8,128)S(1)} %constant_dynamic-update-slice_fusion, f32[512,4,512]{0,2,1:T(8,128)S(1)} %copy-done, pred[4]{0:T(512)(128)(4,1)S(1)} %get-tuple-element.34, pred[512,512]{0,1:T(8,128)(4,1)S(1)} %copy-done.5, pred[4]{0:T(512)(128)(4,1)S(1)} %get-tuple-element.35), kind=kOutput, calls=%fused_computation.28 | convolution fusion | flops 3224371200 | bytes 7077896 | tf_op jit(solution)/shard_map/ikj,kjn->in/dot_general | solution.py:44
  343.8 1.3 convolution_add_fusion
  345.1 0.0 all-reduce.15.cloned.1.call-update
  345.1 0.0 all-reduce.19.cloned.1.call-start
  345.2 0.2 copy.16
  345.4 117.3 %all-reduce.15.cloned.1.call-done = (f32[256,256]{1,0:T(8,128)}, f32[4,512,256]{1,2,0:T(8,128)}) async-done(((f32[256,256]{1,0:T(8,128)}, f32[4,512,256]{1,2,0:T(8,128)}), (f32[256,256]{1,0:T(8,128)}, f32[4,512,256]{1,2,0:T(8,128)})) %all-reduce.15.cloned.1.call-update) | async-done | bytes 2359312 | tf_op jit(solution)/shard_map/psum | solution.py:50
  462.7 2.0 bitcast_add_fusion.1
  464.7 0.0 all-reduce.19.cloned.1.call-update
  464.7 0.3 all-reduce.13.cloned.1.call-start
  465.0 71.5 %all-reduce.19.cloned.1.call-done = (f32[256,256]{1,0:T(8,128)}, f32[512,256]{0,1:T(8,128)}) async-done(((f32[256,256]{1,0:T(8,128)}, f32[512,256]{0,1:T(8,128)}), (f32[256,256]{1,0:T(8,128)}, f32[512,256]{0,1:T(8,128)})) %all-reduce.19.cloned.1.call-update) | async-done | bytes 786448 | tf_op jit(solution)/shard_map/psum | solution.py:55
  536.5 1.8 fusion.24
  538.3 1.4 select_bitcast_fusion.3
  539.7 0.0 all-reduce.13.cloned.1.call-update
  539.8 7.3 %bitcast_add_fusion = f32[512,4,512]{0,2,1:T(8,128)} fusion(pred[512,4,512]{2,0,1:T(32,128)(4,1)S(1)} %copy.5, f32[512,4,512]{2,1,0:T(4,128)} %param.2, f32[512,4,512]{0,2,1:T(8,128)} %copy.3, pred[4]{0:T(512)(128)(4,1)S(1)} %get-tuple-element.34, pred[512,512]{0,1:T(8,128)(4,1)S(1)} %copy-done.6, pred[4]{0:T(512)(128)(4,1)S(1)} %get-tuple-element.35), kind=kLoop, calls=%fused_computation.12 | loop fusion | flops 5242880 | bytes 13893640 | tf_op jit(solution)/shard_map/add | solution.py:61
  547.1 5.4 copy.19
  552.5 106.7 %all-reduce.13.cloned.1.call-done = (f32[1,512,256]{1,2,0:T(8,128)}, f32[1,512,256]{1,2,0:T(8,128)}, f32[1,512,256]{1,2,0:T(8,128)}, f32[1,512,256]{1,2,0:T(8,128)}) async-done(((f32[1,512,256]{1,2,0:T(8,128)}, f32[1,512,256]{1,2,0:T(8,128)}, f32[1,512,256]{1,2,0:T(8,128)}, f32[1,512,256]{1,2,0:T(8,128)}), (f32[1,512,256]{1,2,0:T(8,128)}, f32[1,512,256]{1,2,0:T(8,128)}, f32[1,512,256]{1,2,0:T(8,128)}, ...) | async-done | bytes 2097168 | tf_op jit(solution)/shard_map/psum | solution.py:9
  659.3 0.0 copy-done.2
  659.3 10.2 %subtract_select_fusion = f32[512,4,512]{2,0,1:T(8,128)S(1)} fusion(f32[512,4,512]{2,0,1:T(8,128)} %copy.19, pred[4]{0:T(512)(128)(4,1)S(1)} %get-tuple-element.33, f32[4,512,256]{1,2,0:T(8,128)S(1)} %copy-done.2, f32[1,512,256]{1,2,0:T(8,128)} %get-tuple-element.21, f32[1,512,256]{1,2,0:T(8,128)} %get-tuple-element.22, ...), kind=kOutput, calls=%fused_computation.13 | convolution fusion | flops 6449266688 | bytes 13631492 | tf_op jit(solution)/shard_map/in,kjn->ikj/dot_general | solution.py:60
  669.4 4.7 copy.20
  (18 shorter events, 0.2 us)
Async XLA Ops:
  6.5 140.2 %all-reduce.11.cloned.1.call-start = ((), (), s32[]{:S(2)}) async-start(), calls=%async_computation | async-start | bytes 524288 | tf_op jit(solution)/shard_map/psum | solution.py:30
  31.0 299.0 %all-reduce.17.cloned.1.call-start = ((), (), s32[]{:S(2)}) async-start(), calls=%async_computation.3 | async-start | bytes 4194304 | tf_op jit(solution)/shard_map/psum | solution.py:9
  210.0 0.7 copy-start.3
  212.2 250.5 %all-reduce.15.cloned.1.call-start = ((), (), s32[]{:S(2)}) async-start(), calls=%async_computation.2 | async-start | bytes 4718592 | tf_op jit(solution)/shard_map/psum | solution.py:50
  330.0 6.7 copy-start
  330.0 6.7 copy-start.5
  334.7 9.0 %copy-start.1 = (f32[4,512,256]{1,2,0:T(8,128)}, f32[4,512,256]{1,2,0:T(8,128)S(1)}, u32[]{:S(2)}) copy-start(f32[4,512,256]{1,2,0:T(8,128)S(1)} %constant_dynamic-update-slice_fusion) | copy-start | bytes 6291460
  336.6 7.1 %copy-start.4 = (f32[512,128]{0,1:T(8,128)S(1)}, f32[512,128]{0,1:T(8,128)}, u32[]{:S(2)}) copy-start(f32[512,128]{0,1:T(8,128)} %copy-done.3) | copy-start | bytes 786436
  345.1 191.4 %all-reduce.19.cloned.1.call-start = ((), (), s32[]{:S(2)}) async-start(), calls=%async_computation.4 | async-start | bytes 1572864 | tf_op jit(solution)/shard_map/psum | solution.py:55
  462.7 77.1 %copy-start.6 = (pred[512,512]{0,1:T(8,128)(4,1)S(1)}, pred[512,512]{0,1:T(8,128)(4,1)}, u32[]{:S(2)}) copy-start(pred[512,512]{0,1:T(8,128)(4,1)} %iota_compare_fusion.1) | copy-start | bytes 786436
  464.7 194.6 %all-reduce.13.cloned.1.call-start = ((), (), s32[]{:S(2)}) async-start(), calls=%async_computation.1 | async-start | bytes 4194304 | tf_op jit(solution)/shard_map/psum | solution.py:9
  547.1 112.2 %copy-start.2 = (f32[4,512,256]{1,2,0:T(8,128)S(1)}, f32[4,512,256]{1,2,0:T(8,128)}, u32[]{:S(2)}) copy-start(f32[4,512,256]{1,2,0:T(8,128)} %copy-done.1) | copy-start | bytes 6291460
Sparse Core Ops, SparseCore 0:
  31.1 115.5 all-reduce.10
  212.3 117.6 all-reduce.16
  345.2 117.4 all-reduce.14
  465.1 71.3 all-reduce.18
  539.9 119.3 all-reduce.12
where the time goes:
time: 691 us; the launch traced here: 681 us
  waiting for transfers between devices  509 us (74%)
  other arithmetic  68.3 us (10%)
  matrix products  35.1 us (5%)
  local copies, waits for them, and re-layouts  29.3 us (4%)
  blocking collectives  23.1 us (3%)
  between operations  15 us (2%)
    psum x2, waiting for transfers between devices, from_root(): return lax.psum(block, axis)  205 us
    psum x1, waiting for transfers between devices, body(): col_sums, coupling_rows = lax.psum((col_terms, coupling_part), 'row')  117 us
    psum x1, waiting for transfers between devices, body(): gram = lax.psum(gram, 'row')  116 us
    psum x1, waiting for transfers between devices, body(): product, coupling = lax.psum((row_terms, coupling_rows), 'col')  71.5 us
    another operation x6, other arithmetic, body(): factor = jnp.linalg.cholesky(gram)  34 us
    all_gather x1, blocking collectives, body(): rows_panel = lax.all_gather(panel, 'col', axis=1, tiled=True)  23.1 us
    another operation x3, other arithmetic, body(): lax.linalg.triangular_solve(factor, rows_panel, left_side=False, lower=Tr...  19.7 us
  transfers between devices with their start and end apart: 5, of which 5 were waited for; matrix products, arithmetic and copies ran while one was open for 5% of the time, Pallas kernels for 0%

commit v1 on v0

v1 whole, which is shorter than its diff:
```python
import functools

import jax
import jax.numpy as jnp
from jax import lax
from jax.experimental import pallas as pl
from jax.experimental.pallas import tpu as pltpu
from jax.sharding import PartitionSpec as P

F32 = jnp.float32
BF16 = jnp.bfloat16
HIGHEST = lax.Precision.HIGHEST
MESH = pl.DeviceIdType.MESH
TILE = 512
K = 256
SLOTS = 4
CHUNK = 64
WIDE = 80
NN = (((1,), (0,)), ((), ()))
NT = (((1,), (1,)), ((), ()))


def split(value):
    high = value.astype(BF16)
    return high, (value - high.astype(F32)).astype(BF16)


def dot3(left, right, dims=NN):
    (lh, ll), (rh, rl) = left, right
    dot = functools.partial(lax.dot_general, dimension_numbers=dims, preferred_element_type=F32)
    return dot(lh, rh) + (dot(lh, rl) + dot(ll, rh))


def dot6(left, right, dims=NN):
    return lax.dot_general(left, right, dims, precision=HIGHEST, preferred_element_type=F32)


def mod(value, size):
    return lax.rem(value, size)


class Place:
    def __init__(self):
        self.row = lax.axis_index("row")
        self.col = lax.axis_index("col")
        self.x = lax.div(self.row, 8)
        self.inner = mod(self.row, 8)
        self.y = lax.div(self.inner, 2)
        self.core = mod(self.row, 2)
        self.u = self.y * (1 - self.core) + self.x * self.core
        self.v = self.x * (1 - self.core) + self.y * self.core

    def ring(self, du, dv):
        u, v = mod(self.u + du, 4), mod(self.v + dv, 4)
        return (8 * v + 2 * u) * (1 - self.core) + (8 * u + 2 * v + 1) * self.core

    def at(self, du, dv):
        return {"row": self.ring(du, dv), "col": self.col}

    def sibling(self):
        return {"row": self.row + 1 - 2 * self.core, "col": self.col}

    def up(self, dz):
        return {"row": self.row, "col": mod(self.col + dz % 8, 8)}


class Links:
    def __init__(self, send, recv):
        self.send, self.recv = send, recv
        self.sent, self.slots = 0, 0
        self.pending = []

    def slot(self):
        self.slots += 1
        return self.slots - 1

    def copy(self, source, target, slot, device, send=0):
        return pltpu.make_async_remote_copy(
            src_ref=source,
            dst_ref=target,
            send_sem=self.send.at[send],
            recv_sem=self.recv.at[slot],
            device_id=device,
            device_id_type=MESH,
        )

    def start(self, source, target, slot, device, when=None):
        copy = self.copy(source, target, slot, device, self.sent)
        self.sent += 1
        if when is None:
            copy.start()
        else:
            pl.when(when)(copy.start)
        self.pending.append((copy, when))

    def wait(self, target, slot, device, when=None):
        copy = self.copy(target, target, slot, device)
        if when is None:
            copy.wait_recv()
        else:
            pl.when(when)(copy.wait_recv)

    def finish(self):
        for copy, when in self.pending:
            if when is None:
                copy.wait_send()
            else:
                pl.when(when)(copy.wait_send)
        self.pending = []


def plane_gather(place, links, buf, rows):
    first, second = pl.ds(0, rows // 2), pl.ds(rows // 2, rows // 2)
    near = {name: links.slot() for name in ("l", "r", "a", "b")}
    far = [{name: links.slot() for name in ("l", "r", "a", "b")} for _ in range(4)]
    across = [[links.slot() for _ in range(4)] for _ in range(4)]

    def whole(du, dv):
        return buf.at[place.ring(du, dv)]

    def half(du, dv, part):
        return buf.at[place.ring(du, dv), part]

    def send(ref, slot, du, dv):
        links.start(ref, ref, slot, place.at(du, dv))

    def to_sibling(du, dv):
        links.start(whole(du, dv), whole(du, dv), across[du][dv], place.sibling())

    def spread(du):
        send(whole(du, 0), far[du]["l"], 0, 1)
        send(whole(du, 0), far[du]["r"], 0, 3)
        to_sibling(du, 0)

    def middle(du):
        links.wait(whole(du, 3), far[du]["l"], place.at(0, 3))
        send(half(du, 3, first), far[du]["a"], 0, 1)
        to_sibling(du, 3)
        links.wait(whole(du, 1), far[du]["r"], place.at(0, 1))
        send(half(du, 1, second), far[du]["b"], 0, 3)
        to_sibling(du, 1)

    send(whole(0, 0), near["l"], 1, 0)
    send(whole(0, 0), near["r"], 3, 0)
    spread(0)
    yield
    links.wait(whole(3, 0), near["l"], place.at(3, 0))
    send(half(3, 0, first), near["a"], 1, 0)
    links.wait(whole(1, 0), near["r"], place.at(1, 0))
    send(half(1, 0, second), near["b"], 3, 0)
    spread(3)
    spread(1)
    yield
    middle(0)
    yield
    links.wait(half(2, 0, first), near["a"], place.at(3, 0))
    links.wait(half(2, 0, second), near["b"], place.at(1, 0))
    spread(2)
    yield
    middle(3)
    middle(1)
    yield
    middle(2)
    yield
    for du in (0, 3, 1, 2):
        links.wait(half(du, 2, first), far[du]["a"], place.at(0, 3))
        links.wait(half(du, 2, second), far[du]["b"], place.at(0, 1))
        to_sibling(du, 2)
    yield
    su = place.v
    sv = place.u
    for du in range(4):
        for dv in range(4):
            u, v = mod(su + du, 4), mod(sv + dv, 4)
            chunk = (8 * v + 2 * u) * place.core + (8 * u + 2 * v + 1) * (1 - place.core)
            links.wait(buf.at[chunk], across[du][dv], place.sibling())


def ring_gather(place, links, buf):
    rows = buf.shape[1]
    part = (pl.ds(0, rows // 2), pl.ds(rows // 2, rows // 2))
    slots = [(links.slot(), links.slot()) for _ in range(4)]

    def ref(offset, which, step):
        chunk = mod(place.col + offset % 8, 8)
        return buf.at[chunk, part[which]] if step == 3 else buf.at[chunk]

    for step in range(4):
        for which, way in ((0, 1), (1, 7)):
            if step:
                links.wait(ref(-way * step, which, step - 1), slots[step - 1][which], place.up(-way))
            source = ref(-way * step, which, step)
            links.start(source, source, slots[step][which], place.up(way))
        yield
    for which, way in ((0, 1), (1, 7)):
        links.wait(ref(4, which, 3), slots[3][which], place.up(-way))


def ring_sum(place, links, buf, land):
    rows = buf.shape[1]
    part = (pl.ds(0, rows // 2), pl.ds(rows // 2, rows // 2))
    slots = [(links.slot(), links.slot()) for _ in range(4)]
    for step in range(5):
        for which, way in ((0, 1), (1, 7)):
            chunk = mod(place.col + way * (4 - step) % 8, 8)
            if step:
                spot = land.at[which, step - 1, part[which]] if step == 1 else land.at[which, step - 1]
                links.wait(spot, slots[step - 1][which], place.up(-way))
                if step == 1:
                    buf[chunk, part[which]] += spot[...]
                else:
                    buf[chunk] += spot[...]
            if step < 4:
                source = buf.at[chunk, part[which]] if step == 0 else buf.at[chunk]
                spot = land.at[which, step, part[which]] if step == 0 else land.at[which, step]
                links.start(source, spot, slots[step][which], place.up(way))
        if step < 4:
            yield


def sibling_send(place, links, buf, land, slots, tile):
    for y in range(4):
        links.start(
            buf.at[8 * tile + 2 * y + 1 - place.core],
            land.at[4 * tile + y],
            slots[4 * tile + y],
            place.sibling(),
        )


def plane_sum(place, links, buf, sib, sib_slots, rb, rw, cb, cw):
    rows = buf.shape[1]
    part = (pl.ds(0, rows // 2), pl.ds(rows // 2, rows // 2))
    vb = [(links.slot(), links.slot()) for _ in range(4)]
    vw = [(links.slot(), links.slot()) for _ in range(4)]
    ub = (links.slot(), links.slot())
    uw = (links.slot(), links.slot())
    for index in range(16):
        links.wait(sib.at[index], sib_slots[index], place.sibling())

        buf[8 * (index // 4) + 2 * (index % 4) + place.core] += sib[index]
    order = (2, 1, 3, 0)
    for du in order:
        for which, way in ((0, 1), (1, 3)):
            links.start(
                buf.at[place.ring(du, 2), part[which]], rb.at[du, part[which]], vb[du][which], place.at(0, way)
            )
    yield
    for du in order:
        for which, way in ((0, 1), (1, 3)):
            links.wait(rb.at[du, part[which]], vb[du][which], place.at(0, 4 - way))
            chunk = place.ring(du, way)
            buf[chunk, part[which]] += rb[du, part[which]]
            links.start(buf.at[chunk], rw.at[which, du], vw[du][which], place.at(0, way))
    yield
    for du in order:
        for which, way in ((0, 1), (1, 3)):
            links.wait(rw.at[which, du], vw[du][which], place.at(0, 4 - way))
        chunk = place.ring(du, 0)
        buf[chunk] += rw[0, du] + rw[1, du]
        if du == 2:
            for which, way in ((0, 1), (1, 3)):
                links.start(buf.at[chunk, part[which]], cb.at[part[which]], ub[which], place.at(way, 0))
    yield
    for which, way in ((0, 1), (1, 3)):
        links.wait(cb.at[part[which]], ub[which], place.at(4 - way, 0))
        chunk = place.ring(way, 0)
        buf[chunk, part[which]] += cb[part[which]]
        links.start(buf.at[chunk], cw.at[which], uw[which], place.at(way, 0))
    yield
    for which, way in ((0, 1), (1, 3)):
        links.wait(cw.at[which], uw[which], place.at(4 - way, 0))
    buf[place.ring(0, 0)] += cw[0] + cw[1]


def unpack(pieces):
    lane = lax.broadcasted_iota(jnp.int32, (16, 128), 1) // 32
    bands = []
    for quarter in range(4):
        sides = []
        for side in range(2):
            out = None
            for group in range(4):
                piece = pieces[4 * side + group]
                shift = (group - quarter) * 32 % 128
                piece = pltpu.roll(piece, shift, 1) if shift else piece
                out = piece if out is None else jnp.where(lane == group, piece, out)
            sides.append(out)
        bands.append(jnp.concatenate(sides, 1))
    return jnp.concatenate(bands, 0)


def exchange_kernel(
    stored,
    panel,
    acol_hi_out,
    acol_lo_out,
    arow_hi_out,
    arow_lo_out,
    ycol_out,
    yrow_out,
    s,
    pk,
    colpk,
    rowpk,
    acol,
    arow,
    acol_hi,
    acol_lo,
    arow_hi,
    arow_lo,
    rows,
    diag,
    part,
    sib,
    rb,
    rw,
    cb,
    cw,
    zland,
    turned,
    small,
    ycol,
    yrow,
    load_sem,
    out_sem,
    send_sem,
    recv_sem,
):
    place = Place()
    links = Links(send_sem, recv_sem)
    row, col, inner = place.row, place.col, place.inner
    base = row - inner
    loads = [pltpu.make_async_copy(stored.at[:, k, :], s.at[k], load_sem.at[k]) for k in range(SLOTS)]
    for load in loads:
        load.start()

    barrier = pltpu.get_barrier_semaphore()

    def greet(device):
        pl.semaphore_signal(barrier, inc=1, device_id=device, device_id_type=MESH)

    own = inner == col
    turn = {"row": base + col, "col": inner}
    for step in range(1, 8):
        greet(place.up(step))
        greet({"row": base + mod(inner + step, 8), "col": inner})
        greet({"row": base + col, "col": mod(col + step, 8)})
    for device in (place.at(1, 0), place.at(3, 0), place.at(0, 1), place.at(0, 3), place.sibling()):
        greet(device)

    @pl.when(jnp.logical_not(own))
    def _():
        greet({"row": row, "col": inner})
        greet({"row": base + col, "col": col})

    for index in range(8):
        start = index * CHUNK
        pk[index] = jnp.concatenate(
            [panel[start + 16 * quarter : start + 16 * (quarter + 1), :] for quarter in range(4)], 1
        )
    other = jnp.logical_not(own)
    pl.when(own)(lambda: pl.semaphore_wait(barrier, 26))
    pl.when(other)(lambda: pl.semaphore_wait(barrier, 28))

    col_slot = links.slots
    row_slot = links.slots + 8
    links.slots += 16
    for step in range(8):
        piece = mod(inner + step, 8)
        links.start(
            pk.at[piece],
            colpk.at[col],
            col_slot + col,
            {"row": base + piece, "col": inner},
            None if step else other,
        )
    for step in range(1, 8):
        piece = mod(col + step, 8)
        links.start(pk.at[piece], rowpk.at[col], row_slot + col, place.up(step))
    rowpk[col] = pk[col]

    @pl.when(own)
    def _():
        colpk[col] = pk[inner]

    for step in range(8):
        piece = mod(col + step, 8)
        device = {"row": base + col, "col": piece}
        links.wait(colpk.at[piece], col_slot + piece, device, None if step else other)
        if step:
            links.wait(rowpk.at[piece], row_slot + piece, place.up(step))
    acol[row] = unpack([colpk[index] for index in range(8)])
    arow[col] = unpack([rowpk[index] for index in range(8)])

    wide = plane_gather(place, links, acol, CHUNK)
    deep = ring_gather(place, links, arow)
    next(wide)
    next(deep)
    chunk = acol[row]
    gram = dot6(chunk.T, chunk)
    part[:, CHUNK : CHUNK + 8, :] = gram.reshape(32, 8, K)
    next(wide)
    next(deep)
    for load in loads:
        load.wait()

    @pl.when(own)
    def _():
        value = s[place.x]
        below = lax.broadcasted_iota(jnp.int32, (TILE, TILE), 0)
        across = lax.broadcasted_iota(jnp.int32, (TILE, TILE), 1)
        s[place.x] = jnp.where(below >= across, value, 0.0) + jnp.where(below > across, value, 0.0).T

    next(wide)
    next(deep)
    next(wide)
    next(deep)
    for _ in deep:
        pass
    for _ in wide:
        pass

    def store_halves(source, high, low, outs, sems):
        high[...], low[...] = split(source[...])
        copies = [pltpu.make_async_copy(ref, out, out_sem.at[sem]) for ref, out, sem in zip((high, low), outs, sems)]
        for copy in copies:
            copy.start()
        return copies

    copies = store_halves(arow, arow_hi, arow_lo, (arow_hi_out, arow_lo_out), (0, 1))
    copies += store_halves(acol, acol_hi, acol_lo, (acol_hi_out, acol_lo_out), (2, 3))

    rows[...] = jnp.zeros_like(rows)
    diag[...] = jnp.zeros_like(diag)

    def row_terms(k, carry):
        @pl.when(8 * k + col < row)
        def _():
            right = [ref[pl.ds(8 * k, 8)].reshape(TILE, K) for ref in (acol_hi, acol_lo)]
            rows[...] += dot3(split(s[k]), right).reshape(rows.shape)

        return carry

    lax.fori_loop(0, SLOTS, row_terms, 0)
    arow_halves = [ref[...].reshape(TILE, K) for ref in (arow_hi, arow_lo)]

    @pl.when(own)
    def _():
        diag[...] = dot3(split(s[place.x]), arow_halves).reshape(diag.shape)

    terms = (rows[...] + 0.5 * diag[...]).reshape(TILE, K)
    lower = dot3(split(arow[...].reshape(TILE, K).T), split(terms))
    part[:, CHUNK + 8 :, :] = lower.reshape(32, 8, K)
    rows[...] += diag[...]

    deep = ring_sum(place, links, rows, zland)
    next(deep)
    sib_slots = [links.slot() for _ in range(16)]
    for k in range(SLOTS):
        part[8 * k : 8 * k + 8, :CHUNK, :] = jnp.zeros((8, CHUNK, K), F32)

        @pl.when(8 * k + col < row)
        def _():
            terms = dot3(split(s[k].T), [ref[...].reshape(TILE, K) for ref in (arow_hi, arow_lo)])
            part[8 * k : 8 * k + 8, :CHUNK, :] = terms.reshape(8, CHUNK, K)

        sibling_send(place, links, part, sib, sib_slots, k)
        if k < SLOTS - 1:
            next(deep)
    wide = plane_sum(place, links, part, sib, sib_slots, rb, rw, cb, cw)
    next(wide)
    for _ in deep:
        pass

    turn_slot = links.slot()
    links.start(rows.at[col], turned, turn_slot, turn, other)

    @pl.when(own)
    def _():
        turned[...] = rows[col]

    for _ in wide:
        pass
    small_slot = links.slots
    links.slots += 8
    small[col] = part[row, CHUNK:, :]
    for step in range(1, 8):
        links.start(part.at[row, pl.ds(CHUNK, 16)], small.at[col], small_slot + col, place.up(step))
    links.wait(turned, turn_slot, turn, other)
    product = part[row, :CHUNK, :] + turned[...]
    ycol[row, :CHUNK, :] = product
    back_slot = links.slot()
    links.start(ycol.at[row, pl.ds(0, CHUNK)], yrow.at[inner], back_slot, turn, other)

    @pl.when(own)
    def _():
        yrow[inner] = product

    for step in range(1, 8):
        piece = mod(col + step, 8)
        links.wait(small.at[piece], small_slot + piece, place.up(step))
    ycol[row, CHUNK:, :] = jnp.sum(small[...], 0)
    wide = plane_gather(place, links, ycol, WIDE)
    deep = ring_gather(place, links, yrow)
    next(wide)
    links.wait(yrow.at[col], back_slot, turn, other)
    next(deep)
    next(wide)
    next(deep)
    next(wide)
    next(deep)
    next(wide)
    next(deep)
    for _ in deep:
        pass
    for _ in wide:
        pass
    copies += [
        pltpu.make_async_copy(ref, out, out_sem.at[sem])
        for ref, out, sem in ((ycol, ycol_out, 4), (yrow, yrow_out, 5))
    ]
    copies[-2].start()
    copies[-1].start()
    for copy in copies:
        copy.wait()
    links.finish()


def update_kernel(
    stored, acol_hi, acol_lo, arow_hi, arow_lo, ycol, yrow, out, s, ah, al, rh, rl, yc, yr, gn, inv, scaled_ref, load_sem, out_sem
):
    row, col = lax.axis_index("row"), lax.axis_index("col")
    first = pltpu.make_async_copy(ycol.at[:, pl.ds(CHUNK, 16), :], gn, load_sem.at[0])
    first.start()
    loads = [
        pltpu.make_async_copy(source, target, load_sem.at[index + 1])
        for index, (source, target) in enumerate(
            [(yrow, yr), (arow_hi, rh), (arow_lo, rl), (ycol.at[:, pl.ds(0, CHUNK), :], yc), (acol_hi, ah), (acol_lo, al)]
            + [(stored.at[:, k, :], s.at[k]) for k in range(SLOTS)]
        )
    ]
    for load in loads:
        load.start()
    first.wait()
    gram = gn[:, :8, :].reshape(K, K)
    lower = gn[:, 8:, :].reshape(K, K)
    across = lax.broadcasted_iota(jnp.int32, (K, K), 1)
    eye = lax.broadcasted_iota(jnp.int32, (K, K), 0) == across
    diagonal = jnp.where(eye, gram, 0.0)
    left = lax.rsqrt(jnp.sum(diagonal, 1, keepdims=True))
    right = lax.rsqrt(jnp.sum(diagonal, 0, keepdims=True))
    scaled = gram * left * right
    unit = jnp.where(eye, 1.0, 0.0)
    rest = unit - scaled
    square = dot3(split(rest), split(rest))
    close = jnp.sum(square * square) < 0.25
    bound = jnp.max(jnp.sum(jnp.abs(scaled), 1, keepdims=True))
    inv[...] = jnp.where(close, unit + rest, unit / bound)
    scaled_ref[...] = scaled

    def again(state):
        count, size = state
        return (count < 64) & (size > 1e-6)

    def refine(state):
        count, _ = state
        value = inv[...]
        rest = unit - dot6(scaled_ref[...], value)
        inv[...] = value + dot3(split(value), split(rest))
        return count + 1, jnp.sum(rest * rest)

    lax.while_loop(again, refine, (jnp.int32(0), jnp.float32(1.0)))
    inverse = inv[...] * left * right
    coupling = lower + lower.T
    halves = split(inverse)
    twist = dot3(halves, split(dot3(split(coupling), halves)))
    mix = split(jnp.concatenate([2.0 * inverse, -2.0 * twist], 0))
    for load in loads[:3]:
        load.wait()
    row_halves = rh[...], rl[...]
    yr_halves = split(yr[...].reshape(TILE, K))
    row_halves = [ref[...].reshape(TILE, K) for ref in (rh, rl)]
    wrow = split(dot3([jnp.concatenate(pair, 1) for pair in zip(yr_halves, row_halves)], mix))
    left_pair = [jnp.concatenate(pair, 1) for pair in zip(row_halves, wrow)]
    for load in loads[3:6]:
        load.wait()
    stores = []
    for k in range(SLOTS):
        loads[6 + k].wait()

        @pl.when(8 * k + col == row)
        def _():
            value = s[k]
            down = lax.broadcasted_iota(jnp.int32, (TILE, TILE), 0)
            along = lax.broadcasted_iota(jnp.int32, (TILE, TILE), 1)
            s[k] = jnp.where(down >= along, value, 0.0) + jnp.where(down > along, value, 0.0).T

        @pl.when(8 * k + col > row)
        def _():
            s[k] = jnp.zeros((TILE, TILE), F32)

        @pl.when(8 * k + col <= row)
        def _():
            y_halves = split(yc[8 * k : 8 * k + 8].reshape(TILE, K))
            a_halves = [ref[8 * k : 8 * k + 8].reshape(TILE, K) for ref in (ah, al)]
            wcol = split(dot3([jnp.concatenate(pair, 1) for pair in zip(y_halves, a_halves)], mix))
            right_pair = [jnp.concatenate(pair, 1) for pair in zip(wcol, a_halves)]
            s[k] -= dot3(left_pair, right_pair, NT)

        stores.append(pltpu.make_async_copy(s.at[k], out.at[:, k, :], out_sem.at[k]))
        stores[-1].start()
    for store in stores:
        store.wait()


def body(stored, panel):
    any_spec = pl.BlockSpec(memory_space=pl.ANY)
    col_bf = jax.ShapeDtypeStruct((32, CHUNK, K), BF16)
    row_bf = jax.ShapeDtypeStruct((8, CHUNK, K), BF16)
    vmem, dma = pltpu.VMEM, pltpu.SemaphoreType.DMA
    outs = (
        col_bf,
        col_bf,
        row_bf,
        row_bf,
        jax.ShapeDtypeStruct((32, WIDE, K), F32),
        jax.ShapeDtypeStruct((8, CHUNK, K), F32),
    )
    parts = pl.pallas_call(
        exchange_kernel,
        out_shape=outs,
        in_specs=[any_spec, pl.BlockSpec(memory_space=pltpu.VMEM)],
        out_specs=[any_spec] * 6,
        scratch_shapes=[
            vmem((SLOTS, TILE, TILE), F32),
            vmem((8, 16, 128), F32),
            vmem((8, 16, 128), F32),
            vmem((8, 16, 128), F32),
            vmem((32, CHUNK, K), F32),
            vmem((8, CHUNK, K), F32),
            vmem((32, CHUNK, K), BF16),
            vmem((32, CHUNK, K), BF16),
            vmem((8, CHUNK, K), BF16),
            vmem((8, CHUNK, K), BF16),
            vmem((8, CHUNK, K), F32),
            vmem((8, CHUNK, K), F32),
            vmem((32, WIDE, K), F32),
            vmem((16, WIDE, K), F32),
            vmem((4, WIDE, K), F32),
            vmem((2, 4, WIDE, K), F32),
            vmem((WIDE, K), F32),
            vmem((2, WIDE, K), F32),
            vmem((2, 4, CHUNK, K), F32),
            vmem((CHUNK, K), F32),
            vmem((8, 16, K), F32),
            vmem((32, WIDE, K), F32),
            vmem((8, CHUNK, K), F32),
            dma((SLOTS,)),
            dma((6,)),
            dma((220,)),
            dma((220,)),
        ],
        compiler_params=pltpu.CompilerParams(
            collective_id=0, has_side_effects=True, vmem_limit_bytes=56 << 20
        ),
        name="exchange",
    )(stored, panel)
    return pl.pallas_call(
        update_kernel,
        out_shape=jax.ShapeDtypeStruct(stored.shape, F32),
        in_specs=[any_spec] * 7,
        out_specs=any_spec,
        scratch_shapes=[
            vmem((SLOTS, TILE, TILE), F32),
            vmem((32, CHUNK, K), BF16),
            vmem((32, CHUNK, K), BF16),
            vmem((8, CHUNK, K), BF16),
            vmem((8, CHUNK, K), BF16),
            vmem((32, CHUNK, K), F32),
            vmem((8, CHUNK, K), F32),
            vmem((32, 16, K), F32),
            vmem((K, K), F32),
            vmem((K, K), F32),
            dma((11,)),
            dma((SLOTS,)),
        ],
        compiler_params=pltpu.CompilerParams(vmem_limit_bytes=56 << 20),
        name="update",
    )(stored, *parts)


def solution(mesh):
    in_specs = (P("row", None, "col"), P("row", "col"))
    out_specs = P("row", None, "col")
    return jax.shard_map(body, mesh=mesh, in_specs=in_specs, out_specs=out_specs, check_vma=False)
```

time: 691 us -> 123 us (0.18); the launches traced: 681 us -> 123 us
  waiting for transfers between devices: 509 us -> 0 us
  Pallas kernels: 0 us -> 121 us
  other arithmetic: 68.3 us -> 0 us
  matrix products: 35.1 us -> 0 us
  local copies, waits for them, and re-layouts: 29.3 us -> 1.67 us
  blocking collectives: 23.1 us -> 0 us
  between operations: 15 us -> 0.17 us
    psum x5 -> x0, waiting for transfers between devices: 509 us -> none  [the longest x2 205 us: from_root(): return lax.psum(block, axis)]
    pallas_call x0 -> x2, Pallas kernels: none -> 121 us  [the longest x1 101 us: body(): pl.pallas_call(exchange_kernel, out_shape=outs, in_specs=[any_spec, pl.Bl...]
    another operation x11 -> x0, other arithmetic: 56.5 us -> none  [the longest x6 34 us: body(): factor = jnp.linalg.cholesky(gram)]
    dot_general x7 -> x0, matrix products: 33.4 us -> none  [the longest x1 10.2 us: body(): update = jnp.einsum('in,kjn->ikj', left_pair, right_pair, precision=highest)]
    all_gather x1 -> x0, blocking collectives: 23.1 us -> none  [body(): rows_panel = lax.all_gather(panel, 'col', axis=1, tiled=True)]
    add x2 -> x0, other arithmetic: 9.33 us -> none  [the longest x1 7.35 us: body(): whole_tiles = lower_part + jnp.swapaxes(strict_diag, 0, 2)]
    unnamed x18 -> x1, local copies, waits for them, and re-layouts: 9.6 us -> 1.67 us
  transfers between devices with their start and end apart: 5 -> 0, of which waited for: 5 -> 0; matrix products, arithmetic and copies ran while one was open for 5% -> 0% of each run, Pallas kernels for 0% -> 0%
where the time goes in v1:
time: 123 us
  Pallas kernels  121 us (98%)
  local copies, waits for them, and re-layouts  1.67 us (1%)
    pallas_call x1, Pallas kernels, body(): pl.pallas_call(exchange_kernel, out_shape=outs, in_specs=[any_spec, pl.Bl...  101 us
    pallas_call x1, Pallas kernels, body(): pl.pallas_call(update_kernel, out_shape=jax.ShapeDtypeStruct(stored.shape...  19.9 us

profile of v1, /device:TPU:7, one launch (start us, length us, event | category | flops | bytes accessed | tf_op | source)
XLA Modules:
  0.0 122.9 jit_solution(5032193462813427700)
XLA Ops:
  0.0 1.7 %copy.3.panel = f32[512,32]{1,0:T(8,128)} copy(f32[512,32]{0,1:T(8,128)} %param.3) | data formatting | bytes 131072 | tf_op args[1]
  1.7 101.2 %exchange.1 = (bf16[32,64,256]{2,1,0:T(8,128)(2,1)}, bf16[32,64,256]{2,1,0:T(8,128)(2,1)}, bf16[8,64,256]{2,1,0:T(8,128)(2,1)}, bf16[8,64,256]{2,1,0:T(8,128)(2,...) custom-call(f32[512,4,512]{2,1,0:T(4,128)} %stored.3, f32[512,32]{1,0:T(8,128)} %copy.3.panel), custom_call_target="tpu_custom_call" | custom-call | tf_op jit(solution)/shard_map/exchange/pallas_call | solution.py:630
  102.9 19.9 %update.1 = f32[512,4,512]{2,1,0:T(4,128)} custom-call(f32[512,4,512]{2,1,0:T(4,128)} %stored.3, bf16[32,64,256]{2,1,0:T(8,128)(2,1)} %get-tuple-element.11.acol_hi, bf16[32,64,256]{2,1,0:T(8,128)(2,1)} %get-tuple-element.12.acol_lo, bf16[8,64,256]{2,1,0:T(8,128)(2,1)} %get-tuple-element.13.arow_hi, bf16[8,64,256]{2,1,0:T(8,128)(2,1)} %get-tuple-element.14.arow_lo, ...), custom_call_target="tpu_custom_call" | custom-call | tf_op jit(solution)/shard_map/update/pallas_call | solution.py:669

commit v2 on v0

v2 whole, which is shorter than its diff:
```python
import functools

import jax
import jax.numpy as jnp
from jax import lax
from jax.experimental import pallas as pl
from jax.experimental.pallas import tpu as pltpu
from jax.sharding import PartitionSpec as P

F32 = jnp.float32
BF16 = jnp.bfloat16
HIGHEST = lax.Precision.HIGHEST
MESH = pl.DeviceIdType.MESH
TILE = 512
K = 256
SLOTS = 4
SENDS, RECVS = 22, 54
CHUNK = 64
NN = (((1,), (0,)), ((), ()))
NT = (((1,), (1,)), ((), ()))


def split(value):
    high = value.astype(BF16)
    return high, (value - high.astype(F32)).astype(BF16)


def dot3(left, right, dims=NN):
    (lh, ll), (rh, rl) = left, right
    dot = functools.partial(lax.dot_general, dimension_numbers=dims, preferred_element_type=F32)
    return dot(lh, rh) + (dot(lh, rl) + dot(ll, rh))


def dot6(left, right, dims=NN):
    return lax.dot_general(left, right, dims, precision=HIGHEST, preferred_element_type=F32)


def mod(value, size):
    return lax.rem(value, size)


class Place:
    def __init__(self):
        self.row = lax.axis_index("row")
        self.col = lax.axis_index("col")
        self.x = lax.div(self.row, 8)
        self.inner = mod(self.row, 8)
        self.y = lax.div(self.inner, 2)
        self.core = mod(self.row, 2)
        self.u = self.y * (1 - self.core) + self.x * self.core
        self.v = self.x * (1 - self.core) + self.y * self.core

    def ring(self, du, dv):
        u, v = mod(self.u + du, 4), mod(self.v + dv, 4)
        return (8 * v + 2 * u) * (1 - self.core) + (8 * u + 2 * v + 1) * self.core

    def at(self, du, dv):
        return {"row": self.ring(du, dv), "col": self.col}

    def sibling(self):
        return {"row": self.row + 1 - 2 * self.core, "col": self.col}

    def up(self, dz):
        return {"row": self.row, "col": mod(self.col + dz % 8, 8)}


class Links:
    def __init__(self, send, recv):
        self.send, self.recv = send, recv
        self.sends, self.slots = 0, 0
        self.ends = []

    def slot(self):
        self.slots += 1
        return self.slots - 1

    def batch(self, ref, when=None):
        self.sends += 1
        self.ends.append((self.sends - 1, ref, when))
        return self.sends - 1

    def copy(self, source, target, slot, device, send):
        return pltpu.make_async_remote_copy(
            src_ref=source,
            dst_ref=target,
            send_sem=self.send.at[send],
            recv_sem=self.recv.at[slot],
            device_id=device,
            device_id_type=MESH,
        )

    def start(self, source, target, slot, device, send=None, when=None):
        send = self.batch(source) if send is None else send
        copy = self.copy(source, target, slot, device, send)
        copy.start() if when is None else pl.when(when)(copy.start)

    def wait(self, ref, slot, device, when=None):
        copy = self.copy(ref, ref, slot, device, 0)
        copy.wait_recv() if when is None else pl.when(when)(copy.wait_recv)

    def finish(self, device):
        for send, ref, when in self.ends:
            copy = self.copy(ref, ref, 0, device, send)
            copy.wait_send() if when is None else pl.when(when)(copy.wait_send)


def plane_gather(place, links, buf):
    near = [None] + [links.slot() for _ in range(3)]
    far = [links.slot() for _ in range(4)]
    across = links.slot()
    batch = links.batch(buf.at[pl.ds(0, 31)])

    def send(du, dv, slot, device):
        ref = buf.at[place.ring(du, dv)]
        links.start(ref, ref, slot, device, batch)

    def spread(du):
        for way in (2, 1, 3):
            send(du, 0, far[du], place.at(0, way))
        send(du, 0, across, place.sibling())

    for way in (2, 1, 3):
        send(0, 0, near[way], place.at(way, 0))
    spread(0)
    yield
    for way in (1, 3, 2):
        links.wait(buf.at[place.ring(4 - way, 0)], near[way], place.at(4 - way, 0))
        spread(4 - way)
        yield
    for du in (0, 3, 1, 2):
        links.wait(buf.at[pl.ds(0, 3)], far[du], place.at(0, 1))
        for way in (1, 3, 2):
            send(du, way, across, place.sibling())
        yield
    links.wait(buf.at[pl.ds(0, 16)], across, place.sibling())


def plane_sum(place, links, buf, sib, vland, uland):
    sib_slots = [links.slot() for _ in range(SLOTS)]
    vs = [links.slot() for _ in range(4)]
    us = links.slot()
    batch = links.batch(buf.at[pl.ds(0, 31)])
    for tile in range(SLOTS):
        for y in range(4):
            links.start(
                buf.at[8 * tile + 2 * y + 1 - place.core],
                sib.at[4 * tile + y],
                sib_slots[tile],
                place.sibling(),
                batch,
            )
        yield
    for tile in range(SLOTS):
        links.wait(sib.at[pl.ds(4 * tile, 4)], sib_slots[tile], place.sibling())
        for y in range(4):
            buf[8 * tile + 2 * y + place.core] += sib[4 * tile + y]
    order = (2, 1, 3, 0)
    for du in order:
        for way in (2, 1, 3):
            links.start(buf.at[place.ring(du, way)], vland.at[du, way - 1], vs[du], place.at(0, way), batch)
    yield
    for du in order:
        links.wait(vland.at[du], vs[du], place.at(0, 1))
        chunk = place.ring(du, 0)
        buf[chunk] += vland[du, 0] + (vland[du, 1] + vland[du, 2])
        if du:
            links.start(buf.at[chunk], uland.at[du - 1], us, place.at(du, 0), batch)
        yield
    links.wait(uland, us, place.at(1, 0))
    buf[place.ring(0, 0)] += uland[0] + (uland[1] + uland[2])


def small_sum(place, links, value, sib, chips, depth, total):
    chip = lax.div(place.row, 2)
    sib_slot, chip_slot, depth_slot, back_slot, last_slot = [links.slot() for _ in range(5)]

    def peer(step):
        index = mod(chip + step, 16)
        return index, {"row": 2 * index + place.core, "col": place.col}

    links.start(value.at[:, 1 - place.core], sib, sib_slot, place.sibling())
    yield
    links.wait(sib, sib_slot, place.sibling())
    for index in range(16):
        chips[index] = value[index, place.core] + sib[index]
    batch = links.batch(chips.at[pl.ds(0, 15)])
    for step in range(1, 16):
        index, device = peer(step)
        links.start(chips.at[index], depth.at[0, chip], chip_slot, device, batch)
    yield
    links.wait(depth.at[0, pl.ds(0, 15)], chip_slot, place.sibling())
    depth[0, chip] = chips[chip]
    depth[1, place.col] = jnp.sum(depth[0], 0)
    batch = links.batch(depth.at[1, pl.ds(0, 7)])
    for step in range(1, 8):
        links.start(depth.at[1, place.col], depth.at[1, place.col], depth_slot, place.up(step), batch)
    yield
    links.wait(depth.at[1, pl.ds(0, 7)], depth_slot, place.up(1))
    total[chip, place.core] = jnp.sum(depth[1, :8], 0)
    own = total.at[chip, place.core]
    batch = links.batch(total.at[pl.ds(0, 15), place.core])
    for step in range(1, 16):
        links.start(own, own, back_slot, peer(step)[1], batch)
    yield
    links.wait(total.at[pl.ds(0, 15), place.core], back_slot, place.sibling())
    links.start(total.at[:, place.core], total.at[:, place.core], last_slot, place.sibling())
    yield
    links.wait(total.at[:, 1 - place.core], last_slot, place.sibling())


def ring_gather(place, links, buf):
    rows = buf.shape[1]
    part = (pl.ds(0, rows // 2), pl.ds(rows // 2, rows // 2))
    one, two, three, four = [(links.slot(), links.slot()) for _ in range(4)]
    wholes, halves = links.batch(buf.at[pl.ds(0, 6)]), links.batch(buf.at[0])
    ways = ((0, 1), (1, -1))

    def piece(offset):
        return buf.at[mod(place.col + offset % 8, 8)]

    def half(offset, which):
        return buf.at[mod(place.col + offset % 8, 8), part[which]]

    for which, way in ways:
        links.start(piece(0), piece(0), two[which], place.up(2 * way), wholes)
    for which, way in ways:
        links.start(piece(0), piece(0), one[which], place.up(way), wholes)
    yield
    for which, way in ways:
        source = piece(-2 * way)
        links.wait(source, two[which], place.up(-2 * way))
        links.start(half(-2 * way, which), half(-2 * way, which), four[which], place.up(2 * way), halves)
        links.start(source, source, three[which], place.up(way), wholes)
    yield
    for which, way in ways:
        links.wait(piece(-way), one[which], place.up(-way))
        links.wait(piece(-3 * way), three[which], place.up(-way))
        links.wait(half(-4 * way, which), four[which], place.up(-2 * way))


def ring_sum(place, links, buf, land, half_land):
    rows = buf.shape[1]
    part = (pl.ds(0, rows // 2), pl.ds(rows // 2, rows // 2))
    one, two, three, four = [(links.slot(), links.slot()) for _ in range(4)]
    wholes, halves = links.batch(buf.at[pl.ds(0, 6)]), links.batch(buf.at[0])
    ways = ((0, 1), (1, -1))

    def piece(offset):
        return mod(place.col + offset % 8, 8)

    for which, way in ways:
        links.start(buf.at[piece(4 * way), part[which]], half_land.at[which], four[which], place.up(2 * way), halves)
        links.start(buf.at[piece(3 * way)], land.at[which, 2], three[which], place.up(way), wholes)
    for which, way in ways:
        links.start(buf.at[piece(way)], land.at[which, 0], one[which], place.up(way), wholes)
    yield
    for which, way in ways:
        links.wait(land.at[which, 2], three[which], place.up(-way))
        links.wait(half_land.at[which], four[which], place.up(-2 * way))
        index = piece(2 * way)
        buf[index] += land[which, 2]
        buf[index, part[which]] += half_land[which]
        links.start(buf.at[index], land.at[which, 1], two[which], place.up(2 * way), wholes)
    yield
    for which, way in ways:
        links.wait(land.at[which, 0], one[which], place.up(-way))
        links.wait(land.at[which, 1], two[which], place.up(-2 * way))
    buf[place.col] += (land[0, 0] + land[1, 0]) + (land[0, 1] + land[1, 1])


class Group:
    def __init__(self, place, links, source, target):
        self.place, self.links, self.source, self.target = place, links, source, target
        self.slot = links.slot()
        self.batch = links.batch(target.at[pl.ds(0, 7)])

    def send(self, index):
        place = self.place
        here = place.inner == index

        @pl.when(here)
        def _():
            self.target[place.inner] = self.source[index]

        device = {"row": place.row - place.inner + index, "col": place.col}
        self.links.start(
            self.source.at[index], self.target.at[place.inner], self.slot, device, self.batch, jnp.logical_not(here)
        )

    def wait(self):
        self.links.wait(self.target.at[pl.ds(0, 7)], self.slot, self.place.sibling())


class Turn:
    def __init__(self, place, links, target, own, other):
        self.place, self.links, self.target, self.own, self.other = place, links, target, own, other
        self.slot = links.slot()
        self.batches = links.batch(target.at[pl.ds(0, 7)], own), links.batch(target.at[pl.ds(0, 8)], other)

    def start(self, source, target, device, when):
        for batch, side in zip(self.batches, (self.own, self.other)):
            if when is None:
                self.links.start(source, target, self.slot, device, batch, side)
            elif side is self.other:
                self.links.start(source, target, self.slot, device, batch, side)

    def wait(self):
        self.links.wait(self.target.at[pl.ds(0, 7)], self.slot, self.place.sibling(), self.own)
        self.links.wait(self.target.at[pl.ds(0, 8)], self.slot, self.place.sibling(), self.other)


def unit_matrix():
    return jnp.where(
        lax.broadcasted_iota(jnp.int32, (K, K), 0) == lax.broadcasted_iota(jnp.int32, (K, K), 1), 1.0, 0.0
    ).astype(F32)


def scale(gram):
    diagonal = gram * unit_matrix()
    left = lax.rsqrt(jnp.sum(diagonal, 1, keepdims=True))
    right = lax.rsqrt(jnp.sum(diagonal, 0, keepdims=True))
    return gram * left * right, left, right


def refine(scaled, inverse):
    rest = unit_matrix() - dot6(scaled, inverse)
    return inverse + dot3(split(inverse), split(rest)), jnp.sum(rest * rest)


def mixing(inverse, lower):
    halves = split(inverse)
    twist = dot3(halves, split(dot3(split(lower + lower.T), halves)))
    return split(jnp.concatenate([2.0 * inverse, -2.0 * twist], 0))


def unpack(pieces):
    lane = lax.broadcasted_iota(jnp.int32, (16, 128), 1) // 32
    bands = []
    for quarter in range(4):
        sides = []
        for side in range(2):
            out = None
            for group in range(4):
                piece = pieces[4 * side + group]
                shift = (group - quarter) * 32 % 128
                piece = pltpu.roll(piece, shift, 1) if shift else piece
                out = piece if out is None else jnp.where(lane == group, piece, out)
            sides.append(out)
        bands.append(jnp.concatenate(sides, 1))
    return jnp.concatenate(bands, 0)


def exchange_kernel(
    stored,
    panel,
    acol_hi_out,
    acol_lo_out,
    arow_hi_out,
    arow_lo_out,
    ycol_out,
    yrow_out,
    gram_out,
    lower_out,
    mix_hi_out,
    mix_lo_out,
    size_out,
    s,
    flat,
    packed,
    colpk,
    acol,
    arow,
    acol_hi,
    acol_lo,
    arow_hi,
    arow_lo,
    rows,
    diag,
    whole,
    swapped,
    zland,
    zhalf,
    part,
    sib,
    vland,
    uland,
    ycol,
    yrow,
    gvalue,
    gsib,
    gchips,
    gdepth,
    gtotal,
    nvalue,
    nsib,
    nchips,
    ndepth,
    ntotal,
    scaled,
    inverse,
    mix_hi,
    mix_lo,
    size,
    load_sem,
    out_sem,
    send_sem,
    recv_sem,
):
    place = Place()
    links = Links(send_sem, recv_sem)
    row, col, inner = place.row, place.col, place.inner
    base = row - inner
    fetch = pltpu.make_async_copy(panel, flat, load_sem.at[SLOTS])
    fetch.start()
    loads = [pltpu.make_async_copy(stored.at[:, k, :], s.at[k], load_sem.at[k]) for k in range(SLOTS)]
    for load in loads:
        load.start()

    barrier = pltpu.get_barrier_semaphore()

    def greet(device):
        pl.semaphore_signal(barrier, inc=1, device_id=device, device_id_type=MESH)

    own = inner == col
    other = jnp.logical_not(own)
    for step in range(1, 8):
        greet({"row": base + mod(inner + step, 8), "col": inner})
        greet({"row": base + col, "col": mod(col + step, 8)})
        greet(place.up(step))
        greet({"row": base + mod(inner + step, 8), "col": col})
    for step in range(1, 16):
        greet({"row": mod(row + 2 * step, 32), "col": col})

    @pl.when(other)
    def _():
        greet({"row": row, "col": inner})
        greet({"row": base + col, "col": col})

    fetch.wait()
    for index in range(8):
        start = index * CHUNK
        packed[col, index] = jnp.concatenate(
            [flat[start + 16 * quarter : start + 16 * (quarter + 1), :] for quarter in range(4)], 1
        )
    pl.when(own)(lambda: pl.semaphore_wait(barrier, 43))
    pl.when(other)(lambda: pl.semaphore_wait(barrier, 45))

    turn = Turn(place, links, colpk, own, other)
    for step in range(8):
        piece = mod(inner + step, 8)
        device = {"row": base + piece, "col": inner}
        turn.start(packed.at[col, piece], colpk.at[col], device, None if step else other)
    deep = ring_gather(place, links, packed)
    next(deep)

    @pl.when(own)
    def _():
        colpk[col] = packed[col, inner]

    for load in loads:
        load.wait()

    @pl.when(own)
    def _():
        value = s[place.x]
        below = lax.broadcasted_iota(jnp.int32, (TILE, TILE), 0)
        across = lax.broadcasted_iota(jnp.int32, (TILE, TILE), 1)
        s[place.x] = jnp.where(below >= across, value, 0.0) + jnp.where(below > across, value, 0.0).T

    next(deep)
    turn.wait()
    acol[row] = unpack([colpk[index] for index in range(8)])
    wide = plane_gather(place, links, acol)
    next(wide)
    chunk = acol[row]
    gvalue[...] = dot6(chunk.T, chunk).reshape(gvalue.shape)
    gsum = small_sum(place, links, gvalue, gsib, gchips, gdepth, gtotal)
    next(gsum)
    for _ in deep:
        pass
    for _ in range(3):
        next(wide)

    def unpack_row(index, carry):
        arow[index] = unpack([packed[piece, index] for piece in range(8)])
        return carry

    lax.fori_loop(0, 8, unpack_row, 0)

    def store_halves(source, high, low, outs, sems):
        high[...], low[...] = split(source[...])
        copies = [pltpu.make_async_copy(ref, out, out_sem.at[sem]) for ref, out, sem in zip((high, low), outs, sems)]
        for copy in copies:
            copy.start()
        return copies

    copies = store_halves(arow, arow_hi, arow_lo, (arow_hi_out, arow_lo_out), (0, 1))
    next(gsum)
    next(wide)

    tall = plane_sum(place, links, part, sib, vland, uland)
    for k in range(SLOTS):
        part[8 * k : 8 * k + 8] = jnp.zeros((8, CHUNK, K), F32)

        @pl.when(8 * k + col < row)
        def _():
            terms = dot3(split(s[k].T), [ref[...].reshape(TILE, K) for ref in (arow_hi, arow_lo)])
            part[8 * k : 8 * k + 8] = terms.reshape(8, CHUNK, K)

        next(tall)
        if k < 3:
            next(wide)
    next(tall)
    next(gsum)
    for _ in wide:
        pass
    copies += store_halves(acol, acol_hi, acol_lo, (acol_hi_out, acol_lo_out), (2, 3))

    rows[...] = jnp.zeros_like(rows)
    diag[...] = jnp.zeros_like(diag)
    group = Group(place, links, whole, swapped)
    for block in range(2):
        chunks = pl.ds(4 * block, 4)
        span = pl.ds(TILE // 2 * block, TILE // 2)

        def row_terms(k, carry):
            @pl.when(8 * k + col < row)
            def _():
                right = [ref[pl.ds(8 * k, 8)].reshape(TILE, K) for ref in (acol_hi, acol_lo)]
                rows[chunks] += dot3(split(s[k, span]), right).reshape(4, CHUNK, K)

            return carry

        lax.fori_loop(0, SLOTS, row_terms, 0)

        @pl.when(own)
        def _():
            right = [ref[...].reshape(TILE, K) for ref in (arow_hi, arow_lo)]
            diag[chunks] = dot3(split(s[place.x, span]), right).reshape(4, CHUNK, K)

        whole[chunks] = rows[chunks] + diag[chunks]
        for index in range(4 * block, 4 * block + 4):
            group.send(index)

    terms = (rows[...] + 0.5 * diag[...]).reshape(TILE, K)
    lower = dot3(split(arow[...].reshape(TILE, K).T), split(terms))
    nvalue[...] = lower.reshape(nvalue.shape)
    nsum = small_sum(place, links, nvalue, nsib, nchips, ndepth, ntotal)
    next(nsum)
    next(gsum)
    next(tall)
    next(nsum)
    group.wait()
    deep = ring_sum(place, links, swapped, zland, zhalf)
    next(deep)
    for _ in range(3):
        next(tall)
    next(gsum)
    next(deep)
    next(nsum)
    for _ in tall:
        pass
    for _ in gsum:
        pass
    scaled[...], left, right = scale(gtotal[...].reshape(K, K))
    rest = unit_matrix() - scaled[...]
    square = dot3(split(rest), split(rest))
    close = jnp.sum(square * square) < 0.25
    bound = jnp.max(jnp.sum(jnp.abs(scaled[...]), 1, keepdims=True))
    inverse[...] = jnp.where(close, unit_matrix() + rest, unit_matrix() / bound)
    for _ in deep:
        pass
    product = part[row] + swapped[col]
    ycol[row] = product

    wide = plane_gather(place, links, ycol)
    next(wide)
    turn = Turn(place, links, yrow, own, other)
    for step in range(8):
        piece = mod(col + step, 8)
        device = {"row": base + col, "col": piece}
        turn.start(ycol.at[row], yrow.at[inner], device, None if step else other)

    @pl.when(own)
    def _():
        yrow[inner] = product

    next(nsum)
    inverse[...], _ = refine(scaled[...], inverse[...])
    for _ in range(3):
        next(wide)
    next(nsum)
    inverse[...], _ = refine(scaled[...], inverse[...])
    next(wide)
    inverse[...], _ = refine(scaled[...], inverse[...])
    next(wide)
    inverse[...], final = refine(scaled[...], inverse[...])
    size[...] = jnp.full(size.shape, final, F32)
    next(wide)
    for _ in nsum:
        pass
    mix_hi[...], mix_lo[...] = mixing(inverse[...] * left * right, ntotal[...].reshape(K, K))
    next(wide)
    turn.wait()
    for _ in wide:
        pass
    ends = ((ycol, ycol_out), (yrow, yrow_out), (gtotal, gram_out), (ntotal, lower_out))
    ends += ((mix_hi, mix_hi_out), (mix_lo, mix_lo_out), (size, size_out))
    last = [pltpu.make_async_copy(ref, out, out_sem.at[4 + index]) for index, (ref, out) in enumerate(ends)]
    for copy in last:
        copy.start()
    for copy in copies + last:
        copy.wait()
    links.finish(place.sibling())


def update_kernel(
    stored,
    acol_hi,
    acol_lo,
    arow_hi,
    arow_lo,
    ycol,
    yrow,
    gram_in,
    lower_in,
    mix_hi,
    mix_lo,
    size_in,
    out,
    s,
    ah,
    al,
    rh,
    rl,
    yc,
    yr,
    gn,
    mh,
    ml,
    size,
    scaled,
    inverse,
    load_sem,
    out_sem,
):
    row, col = lax.axis_index("row"), lax.axis_index("col")
    pairs = [(size_in, size), (mix_hi, mh), (mix_lo, ml), (yrow, yr), (arow_hi, rh), (arow_lo, rl)]
    pairs += [(gram_in, gn.at[0]), (lower_in, gn.at[1])]
    heads = len(pairs)
    for k in range(SLOTS):
        eight = pl.ds(8 * k, 8)
        pairs += [(ref.at[eight], land.at[eight]) for ref, land in ((ycol, yc), (acol_hi, ah), (acol_lo, al))]
        pairs.append((stored.at[:, k, :], s.at[k]))
    loads = [pltpu.make_async_copy(source, land, load_sem.at[index]) for index, (source, land) in enumerate(pairs)]
    for load in loads:
        load.start()
    for load in loads[:heads]:
        load.wait()

    @pl.when(jnp.max(size[...]) > 1e-6)
    def _():
        scaled[...], left, right = scale(gn[0].reshape(K, K))
        bound = jnp.max(jnp.sum(jnp.abs(scaled[...]), 1, keepdims=True))
        inverse[...] = unit_matrix() / bound

        def again(state):
            count, rest = state
            return (count < 64) & (rest > 1e-6)

        def step(state):
            inverse[...], rest = refine(scaled[...], inverse[...])
            return state[0] + 1, rest

        lax.while_loop(again, step, (jnp.int32(0), jnp.float32(1.0)))
        mh[...], ml[...] = mixing(inverse[...] * left * right, gn[1].reshape(K, K))

    mix = mh[...], ml[...]
    yr_halves = split(yr[...].reshape(TILE, K))
    row_halves = [ref[...].reshape(TILE, K) for ref in (rh, rl)]
    wrow = split(dot3([jnp.concatenate(pair, 1) for pair in zip(yr_halves, row_halves)], mix))
    left_pair = [jnp.concatenate(pair, 1) for pair in zip(row_halves, wrow)]
    stores = []
    for k in range(SLOTS):
        for load in loads[heads + 4 * k : heads + 4 * k + 4]:
            load.wait()

        @pl.when(8 * k + col == row)
        def _():
            value = s[k]
            down = lax.broadcasted_iota(jnp.int32, (TILE, TILE), 0)
            along = lax.broadcasted_iota(jnp.int32, (TILE, TILE), 1)
            s[k] = jnp.where(down >= along, value, 0.0) + jnp.where(down > along, value, 0.0).T

        @pl.when(8 * k + col > row)
        def _():
            s[k] = jnp.zeros((TILE, TILE), F32)

        @pl.when(8 * k + col <= row)
        def _():
            y_halves = split(yc[8 * k : 8 * k + 8].reshape(TILE, K))
            a_halves = [ref[8 * k : 8 * k + 8].reshape(TILE, K) for ref in (ah, al)]
            wcol = split(dot3([jnp.concatenate(pair, 1) for pair in zip(y_halves, a_halves)], mix))
            right_pair = [jnp.concatenate(pair, 1) for pair in zip(wcol, a_halves)]
            s[k] -= dot3(left_pair, right_pair, NT)

        stores.append(pltpu.make_async_copy(s.at[k], out.at[:, k, :], out_sem.at[k]))
        stores[-1].start()
    for store in stores:
        store.wait()


def body(stored, panel):
    any_spec = pl.BlockSpec(memory_space=pl.ANY)
    vmem, dma = pltpu.VMEM, pltpu.SemaphoreType.DMA
    col_shape, row_shape, square, wide = (32, CHUNK, K), (8, CHUNK, K), (16, 2, 8, K), (2 * K, K)
    out_types = [(col_shape, BF16)] * 2 + [(row_shape, BF16)] * 2 + [(col_shape, F32), (row_shape, F32)]
    out_types += [(square, F32)] * 2 + [(wide, BF16)] * 2 + [((8, 128), F32)]
    small = [
        vmem(square, F32),
        vmem((16, 8, K), F32),
        vmem((16, 8, K), F32),
        vmem((2, 16, 8, K), F32),
        vmem(square, F32),
    ]
    parts = pl.pallas_call(
        exchange_kernel,
        out_shape=[jax.ShapeDtypeStruct(shape, kind) for shape, kind in out_types],
        in_specs=[any_spec] * 2,
        out_specs=[any_spec] * len(out_types),
        scratch_shapes=[
            vmem((SLOTS, TILE, TILE), F32),
            vmem((TILE, K // 8), F32),
            vmem((8, 8, 16, 128), F32),
            vmem((8, 16, 128), F32),
            vmem(col_shape, F32),
            vmem(row_shape, F32),
            vmem(col_shape, BF16),
            vmem(col_shape, BF16),
            vmem(row_shape, BF16),
            vmem(row_shape, BF16),
            vmem(row_shape, F32),
            vmem(row_shape, F32),
            vmem(row_shape, F32),
            vmem(row_shape, F32),
            vmem((2, 3, CHUNK, K), F32),
            vmem((2, CHUNK // 2, K), F32),
            vmem(col_shape, F32),
            vmem((16, CHUNK, K), F32),
            vmem((4, 3, CHUNK, K), F32),
            vmem((3, CHUNK, K), F32),
            vmem(col_shape, F32),
            vmem(row_shape, F32),
            *small,
            *small,
            vmem((K, K), F32),
            vmem((K, K), F32),
            vmem(wide, BF16),
            vmem(wide, BF16),
            vmem((8, 128), F32),
            dma((SLOTS + 1,)),
            dma((11,)),
            dma((SENDS,)),
            dma((RECVS,)),
        ],
        compiler_params=pltpu.CompilerParams(collective_id=0, has_side_effects=True, vmem_limit_bytes=56 << 20),
        name="exchange",
    )(stored, panel)
    return pl.pallas_call(
        update_kernel,
        out_shape=jax.ShapeDtypeStruct(stored.shape, F32),
        in_specs=[any_spec] * (1 + len(out_types)),
        out_specs=any_spec,
        scratch_shapes=[
            vmem((SLOTS, TILE, TILE), F32),
            vmem(col_shape, BF16),
            vmem(col_shape, BF16),
            vmem(row_shape, BF16),
            vmem(row_shape, BF16),
            vmem(col_shape, F32),
            vmem(row_shape, F32),
            vmem((2, *square), F32),
            vmem(wide, BF16),
            vmem(wide, BF16),
            vmem((8, 128), F32),
            vmem((K, K), F32),
            vmem((K, K), F32),
            dma((24,)),
            dma((SLOTS,)),
        ],
        compiler_params=pltpu.CompilerParams(vmem_limit_bytes=56 << 20),
        name="update",
    )(stored, *parts)


def solution(mesh):
    in_specs = (P("row", None, "col"), P("row", "col"))
    out_specs = P("row", None, "col")
    return jax.shard_map(body, mesh=mesh, in_specs=in_specs, out_specs=out_specs, check_vma=False)
```

time: 691 us -> 104 us (0.15); the launches traced: 681 us -> 102 us
  waiting for transfers between devices: 509 us -> 0 us
  Pallas kernels: 0 us -> 100 us
  other arithmetic: 68.3 us -> 0 us
  matrix products: 35.1 us -> 0 us
  local copies, waits for them, and re-layouts: 29.3 us -> 1.67 us
  blocking collectives: 23.1 us -> 0 us
  between operations: 15 us -> 0.17 us
    psum x5 -> x0, waiting for transfers between devices: 509 us -> none  [the longest x2 205 us: from_root(): return lax.psum(block, axis)]
    pallas_call x0 -> x2, Pallas kernels: none -> 100 us  [the longest x1 79.6 us: body(): pl.pallas_call(exchange_kernel, out_shape=[jax.ShapeDtypeStruct(shape, ki...]
    another operation x11 -> x0, other arithmetic: 56.5 us -> none  [the longest x6 34 us: body(): factor = jnp.linalg.cholesky(gram)]
    dot_general x7 -> x0, matrix products: 33.4 us -> none  [the longest x1 10.2 us: body(): update = jnp.einsum('in,kjn->ikj', left_pair, right_pair, precision=highest)]
    all_gather x1 -> x0, blocking collectives: 23.1 us -> none  [body(): rows_panel = lax.all_gather(panel, 'col', axis=1, tiled=True)]
    add x2 -> x0, other arithmetic: 9.33 us -> none  [the longest x1 7.35 us: body(): whole_tiles = lower_part + jnp.swapaxes(strict_diag, 0, 2)]
    unnamed x18 -> x1, local copies, waits for them, and re-layouts: 9.6 us -> 1.67 us
  transfers between devices with their start and end apart: 5 -> 0, of which waited for: 5 -> 0; matrix products, arithmetic and copies ran while one was open for 5% -> 0% of each run, Pallas kernels for 0% -> 0%
where the time goes in v2:
time: 104 us; the launch traced here: 102 us
  Pallas kernels  100 us (96%)
  local copies, waits for them, and re-layouts  1.67 us (2%)
    pallas_call x1, Pallas kernels, body(): pl.pallas_call(exchange_kernel, out_shape=[jax.ShapeDtypeStruct(shape, ki...  79.6 us
    pallas_call x1, Pallas kernels, body(): pl.pallas_call(update_kernel, out_shape=jax.ShapeDtypeStruct(stored.shape...  20.3 us

profile of v2, /device:TPU:7, one launch (start us, length us, event | category | flops | bytes accessed | tf_op | source)
XLA Modules:
  0.0 101.8 jit_solution(14180246897120382297)
XLA Ops:
  0.0 1.7 %copy.3.panel = f32[512,32]{1,0:T(8,128)} copy(f32[512,32]{0,1:T(8,128)} %param.3) | data formatting | bytes 131072 | tf_op args[1]
  1.7 79.6 %exchange.1 = (bf16[32,64,256]{2,1,0:T(8,128)(2,1)}, bf16[32,64,256]{2,1,0:T(8,128)(2,1)}, bf16[8,64,256]{2,1,0:T(8,128)(2,1)}, bf16[8,64,256]{2,1,0:T(8,128)(2,...) custom-call(f32[512,4,512]{2,1,0:T(4,128)} %stored.3, ...), custom_call_target="tpu_custom_call" | custom-call | tf_op jit(solution)/shard_map/exchange/pallas_call | solution.py:726
  81.3 20.3 %update.1 = f32[512,4,512]{2,1,0:T(4,128)} custom-call(f32[512,4,512]{2,1,0:T(4,128)} %stored.3, bf16[32,64,256]{2,1,0:T(8,128)(2,1)} %get-tuple-element.16.acol_hi, bf16[32,64,256]{2,1,0:T(8,128)(2,1)} %get-tuple-element.17.acol_lo, bf16[8,64,256]{2,1,0:T(8,128)(2,1)} %get-tuple-element.18.arow_hi, bf16[8,64,256]{2,1,0:T(8,128)(2,1)} %get-tuple-element.19.arow_lo, ...), custom_call_target="tpu_custom_call" | custom-call | tf_op jit(solution)/shard_map/update/pallas_call | solution.py:769

commit v3 on v2

--- a/solution.py
+++ b/solution.py
@@ -155,10 +155,18 @@
         for y in range(4):
             buf[8 * tile + 2 * y + place.core] += sib[4 * tile + y]
     order = (2, 1, 3, 0)
-    for du in order:
-        for way in (2, 1, 3):
-            links.start(buf.at[place.ring(du, way)], vland.at[du, way - 1], vs[du], place.at(0, way), batch)
-    yield
+    for core in range(2):
+        for du in order:
+            for way in (2, 1, 3):
+                links.start(
+                    buf.at[place.ring(du, way)],
+                    vland.at[du, way - 1],
+                    vs[du],
+                    place.at(0, way),
+                    batch,
+                    place.core == core,
+                )
+        yield
     for du in order:
         links.wait(vland.at[du], vs[du], place.at(0, 1))
         chunk = place.ring(du, 0)
@@ -333,21 +341,21 @@
     return split(jnp.concatenate([2.0 * inverse, -2.0 * twist], 0))
 
 
+def pack(slab, pieces):
+    low = lax.broadcasted_iota(jnp.int32, (16, 128), 1) < CHUNK
+    for pair in range(4):
+        first, second = [slab[16 * side : 16 * side + 16, 128 * pair : 128 * pair + 128] for side in range(2)]
+        pieces[2 * pair] = jnp.where(low, first, pltpu.roll(second, CHUNK, 1))
+        pieces[2 * pair + 1] = jnp.where(low, pltpu.roll(first, CHUNK, 1), second)
+
+
 def unpack(pieces):
-    lane = lax.broadcasted_iota(jnp.int32, (16, 128), 1) // 32
-    bands = []
-    for quarter in range(4):
-        sides = []
-        for side in range(2):
-            out = None
-            for group in range(4):
-                piece = pieces[4 * side + group]
-                shift = (group - quarter) * 32 % 128
-                piece = pltpu.roll(piece, shift, 1) if shift else piece
-                out = piece if out is None else jnp.where(lane == group, piece, out)
-            sides.append(out)
-        bands.append(jnp.concatenate(sides, 1))
-    return jnp.concatenate(bands, 0)
+    turned = pieces.reshape(128, 128).T
+    return jnp.concatenate([turned[:CHUNK], turned[CHUNK:]], 1)
+
+
+def unpack_row(slabs):
+    return jnp.concatenate([slabs[index, 16 * side : 16 * side + 16, :] for side in range(2) for index in range(8)], 0)
 
 
 def exchange_kernel(
@@ -365,11 +373,11 @@
     mix_lo_out,
     size_out,
     s,
-    flat,
+    slabs,
     packed,
     colpk,
     acol,
-    arow,
+    turned,
     acol_hi,
     acol_lo,
     arow_hi,
@@ -410,7 +418,7 @@
     links = Links(send_sem, recv_sem)
     row, col, inner = place.row, place.col, place.inner
     base = row - inner
-    fetch = pltpu.make_async_copy(panel, flat, load_sem.at[SLOTS])
+    fetch = pltpu.make_async_copy(panel, slabs.at[col], load_sem.at[SLOTS])
     fetch.start()
     loads = [pltpu.make_async_copy(stored.at[:, k, :], s.at[k], load_sem.at[k]) for k in range(SLOTS)]
     for load in loads:
@@ -437,11 +445,7 @@
         greet({"row": base + col, "col": col})
 
     fetch.wait()
-    for index in range(8):
-        start = index * CHUNK
-        packed[col, index] = jnp.concatenate(
-            [flat[start + 16 * quarter : start + 16 * (quarter + 1), :] for quarter in range(4)], 1
-        )
+    pack(slabs[col], packed)
     pl.when(own)(lambda: pl.semaphore_wait(barrier, 43))
     pl.when(other)(lambda: pl.semaphore_wait(barrier, 45))
 
@@ -449,13 +453,13 @@
     for step in range(8):
         piece = mod(inner + step, 8)
         device = {"row": base + piece, "col": inner}
-        turn.start(packed.at[col, piece], colpk.at[col], device, None if step else other)
-    deep = ring_gather(place, links, packed)
+        turn.start(packed.at[piece], colpk.at[col], device, None if step else other)
+    deep = ring_gather(place, links, slabs)
     next(deep)
 
     @pl.when(own)
     def _():
-        colpk[col] = packed[col, inner]
+        colpk[col] = packed[inner]
 
     for load in loads:
         load.wait()
@@ -469,7 +473,7 @@
 
     next(deep)
     turn.wait()
-    acol[row] = unpack([colpk[index] for index in range(8)])
+    acol[row] = unpack(colpk[...])
     wide = plane_gather(place, links, acol)
     next(wide)
     chunk = acol[row]
@@ -481,20 +485,15 @@
     for _ in range(3):
         next(wide)
 
-    def unpack_row(index, carry):
-        arow[index] = unpack([packed[piece, index] for piece in range(8)])
-        return carry
-
-    lax.fori_loop(0, 8, unpack_row, 0)
-
     def store_halves(source, high, low, outs, sems):
-        high[...], low[...] = split(source[...])
+        high[...], low[...] = split(source)
         copies = [pltpu.make_async_copy(ref, out, out_sem.at[sem]) for ref, out, sem in zip((high, low), outs, sems)]
         for copy in copies:
             copy.start()
         return copies
 
-    copies = store_halves(arow, arow_hi, arow_lo, (arow_hi_out, arow_lo_out), (0, 1))
+    turned[...] = unpack_row(slabs[...])
+    copies = store_halves(turned[...].T.reshape(8, CHUNK, K), arow_hi, arow_lo, (arow_hi_out, arow_lo_out), (0, 1))
     next(gsum)
     next(wide)
 
@@ -514,7 +513,7 @@
     next(gsum)
     for _ in wide:
         pass
-    copies += store_halves(acol, acol_hi, acol_lo, (acol_hi_out, acol_lo_out), (2, 3))
+    copies += store_halves(acol[...], acol_hi, acol_lo, (acol_hi_out, acol_lo_out), (2, 3))
 
     rows[...] = jnp.zeros_like(rows)
     diag[...] = jnp.zeros_like(diag)
@@ -543,32 +542,32 @@
             group.send(index)
 
     terms = (rows[...] + 0.5 * diag[...]).reshape(TILE, K)
-    lower = dot3(split(arow[...].reshape(TILE, K).T), split(terms))
+    lower = dot3(split(turned[...]), split(terms))
     nvalue[...] = lower.reshape(nvalue.shape)
     nsum = small_sum(place, links, nvalue, nsib, nchips, ndepth, ntotal)
     next(nsum)
+    next(tall)
     next(gsum)
-    next(tall)
     next(nsum)
     group.wait()
     deep = ring_sum(place, links, swapped, zland, zhalf)
     next(deep)
-    for _ in range(3):
-        next(tall)
     next(gsum)
     next(deep)
     next(nsum)
-    for _ in tall:
-        pass
+    for _ in range(4):
+        next(tall)
     for _ in gsum:
         pass
     scaled[...], left, right = scale(gtotal[...].reshape(K, K))
     rest = unit_matrix() - scaled[...]
     square = dot3(split(rest), split(rest))
-    close = jnp.sum(square * square) < 0.25
+    close = jnp.sum(square * square) < 0.8
     bound = jnp.max(jnp.sum(jnp.abs(scaled[...]), 1, keepdims=True))
     inverse[...] = jnp.where(close, unit_matrix() + rest, unit_matrix() / bound)
     for _ in deep:
+        pass
+    for _ in tall:
         pass
     product = part[row] + swapped[col]
     ycol[row] = product
@@ -597,19 +596,31 @@
     inverse[...], final = refine(scaled[...], inverse[...])
     size[...] = jnp.full(size.shape, final, F32)
     next(wide)
+
+    def keep(ref, out, sem):
+        copies.append(pltpu.make_async_copy(ref, out, out_sem.at[sem]))
+        copies[-1].start()
+
+    def keep_cols(core, sem):
+        for chip in range(16):
+            chunk = 2 * chip + core
+            pltpu.make_async_copy(ycol.at[chunk], ycol_out.at[chunk], out_sem.at[sem]).start()
+        copies.append(pltpu.make_async_copy(ycol.at[pl.ds(0, 16)], ycol_out.at[pl.ds(0, 16)], out_sem.at[sem]))
+
     for _ in nsum:
         pass
     mix_hi[...], mix_lo[...] = mixing(inverse[...] * left * right, ntotal[...].reshape(K, K))
+    ends = ((gtotal, gram_out), (ntotal, lower_out), (mix_hi, mix_hi_out), (mix_lo, mix_lo_out), (size, size_out))
+    for index, (ref, out) in enumerate(ends):
+        keep(ref, out, 4 + index)
     next(wide)
+    keep_cols(place.core, 9)
     turn.wait()
+    keep(yrow, yrow_out, 10)
     for _ in wide:
         pass
-    ends = ((ycol, ycol_out), (yrow, yrow_out), (gtotal, gram_out), (ntotal, lower_out))
-    ends += ((mix_hi, mix_hi_out), (mix_lo, mix_lo_out), (size, size_out))
-    last = [pltpu.make_async_copy(ref, out, out_sem.at[4 + index]) for index, (ref, out) in enumerate(ends)]
-    for copy in last:
-        copy.start()
-    for copy in copies + last:
+    keep_cols(1 - place.core, 11)
+    for copy in copies:
         copy.wait()
     links.finish(place.sibling())
 
@@ -646,20 +657,26 @@
 ):
     row, col = lax.axis_index("row"), lax.axis_index("col")
     pairs = [(size_in, size), (mix_hi, mh), (mix_lo, ml), (yrow, yr), (arow_hi, rh), (arow_lo, rl)]
-    pairs += [(gram_in, gn.at[0]), (lower_in, gn.at[1])]
     heads = len(pairs)
     for k in range(SLOTS):
         eight = pl.ds(8 * k, 8)
         pairs += [(ref.at[eight], land.at[eight]) for ref, land in ((ycol, yc), (acol_hi, ah), (acol_lo, al))]
         pairs.append((stored.at[:, k, :], s.at[k]))
     loads = [pltpu.make_async_copy(source, land, load_sem.at[index]) for index, (source, land) in enumerate(pairs)]
-    for load in loads:
+    ahead = heads + 4
+    for load in loads[:ahead]:
         load.start()
     for load in loads[:heads]:
         load.wait()
+    for load in loads[ahead : ahead + 4]:
+        load.start()
 
     @pl.when(jnp.max(size[...]) > 1e-6)
     def _():
+        for index, source in enumerate((gram_in, lower_in)):
+            load = pltpu.make_async_copy(source, gn.at[index], out_sem.at[index])
+            load.start()
+            load.wait()
         scaled[...], left, right = scale(gn[0].reshape(K, K))
         bound = jnp.max(jnp.sum(jnp.abs(scaled[...]), 1, keepdims=True))
         inverse[...] = unit_matrix() / bound
@@ -684,6 +701,8 @@
     for k in range(SLOTS):
         for load in loads[heads + 4 * k : heads + 4 * k + 4]:
             load.wait()
+        for load in loads[ahead + 4 * k + 4 : ahead + 4 * k + 8]:
+            load.start()
 
         @pl.when(8 * k + col == row)
         def _():
@@ -730,11 +749,11 @@
         out_specs=[any_spec] * len(out_types),
         scratch_shapes=[
             vmem((SLOTS, TILE, TILE), F32),
-            vmem((TILE, K // 8), F32),
-            vmem((8, 8, 16, 128), F32),
+            vmem((8, K // 8, TILE), F32),
+            vmem((8, 16, 128), F32),
             vmem((8, 16, 128), F32),
             vmem(col_shape, F32),
-            vmem(row_shape, F32),
+            vmem((K, TILE), F32),
             vmem(col_shape, BF16),
             vmem(col_shape, BF16),
             vmem(row_shape, BF16),
@@ -759,13 +778,13 @@
             vmem(wide, BF16),
             vmem((8, 128), F32),
             dma((SLOTS + 1,)),
-            dma((11,)),
+            dma((12,)),
             dma((SENDS,)),
             dma((RECVS,)),
         ],
         compiler_params=pltpu.CompilerParams(collective_id=0, has_side_effects=True, vmem_limit_bytes=56 << 20),
         name="exchange",
-    )(stored, panel)
+    )(stored, panel.T)
     return pl.pallas_call(
         update_kernel,
         out_shape=jax.ShapeDtypeStruct(stored.shape, F32),
@@ -785,7 +804,7 @@
             vmem((8, 128), F32),
             vmem((K, K), F32),
             vmem((K, K), F32),
-            dma((24,)),
+            dma((22,)),
             dma((SLOTS,)),
         ],
         compiler_params=pltpu.CompilerParams(vmem_limit_bytes=56 << 20),

time: 104 us -> 98.6 us (0.948); the launches traced: 102 us -> 97.8 us
  Pallas kernels: 100 us -> 97.6 us
  local copies, waits for them, and re-layouts: 1.67 us -> 0 us
    pallas_call x1, Pallas kernels: 79.6 us -> 75.1 us  [body(): pl.pallas_call(exchange_kernel, out_shape=[jax.ShapeDtypeStruct(shape, ki...]
    pallas_call x1, Pallas kernels: 20.3 us -> 22.5 us  [body(): pl.pallas_call(update_kernel, out_shape=jax.ShapeDtypeStruct(stored.shape...]
    unnamed x1 -> x0, local copies, waits for them, and re-layouts: 1.67 us -> none
where the time goes in v3:
time: 98.6 us; the launch traced here: 97.8 us
  Pallas kernels  97.6 us (99%)
    pallas_call x1, Pallas kernels, body(): pl.pallas_call(exchange_kernel, out_shape=[jax.ShapeDtypeStruct(shape, ki...  75.1 us
    pallas_call x1, Pallas kernels, body(): pl.pallas_call(update_kernel, out_shape=jax.ShapeDtypeStruct(stored.shape...  22.5 us

profile of v3, /device:TPU:7, one launch (start us, length us, event | category | flops | bytes accessed | tf_op | source)
XLA Modules:
  0.0 97.8 jit_solution(16515878027050400477)
XLA Ops:
  0.0 75.1 %exchange.1 = (bf16[32,64,256]{2,1,0:T(8,128)(2,1)}, bf16[32,64,256]{2,1,0:T(8,128)(2,1)}, bf16[8,64,256]{2,1,0:T(8,128)(2,1)}, bf16[8,64,256]{2,1,0:T(8,128)(2,...) custom-call(f32[512,4,512]{2,1,0:T(4,128)} %stored.3, ...), custom_call_target="tpu_custom_call" | custom-call | tf_op jit(solution)/shard_map/exchange/pallas_call | solution.py:745
  75.1 22.5 %update.1 = f32[512,4,512]{2,1,0:T(4,128)} custom-call(f32[512,4,512]{2,1,0:T(4,128)} %stored.3, bf16[32,64,256]{2,1,0:T(8,128)(2,1)} %get-tuple-element.16.acol_hi, bf16[32,64,256]{2,1,0:T(8,128)(2,1)} %get-tuple-element.17.acol_lo, bf16[8,64,256]{2,1,0:T(8,128)(2,1)} %get-tuple-element.18.arow_hi, bf16[8,64,256]{2,1,0:T(8,128)(2,1)} %get-tuple-element.19.arow_lo, ...), custom_call_target="tpu_custom_call" | custom-call | tf_op jit(solution)/shard_map/update/pallas_call | solution.py:788

commit v4 on v3

--- a/solution.py
+++ b/solution.py
@@ -104,7 +104,8 @@
             copy.wait_send() if when is None else pl.when(when)(copy.wait_send)
 
 
-def plane_gather(place, links, buf):
+def plane_gather(place, links, buf, kept=None):
+    kept = buf if kept is None else kept
     near = [None] + [links.slot() for _ in range(3)]
     far = [links.slot() for _ in range(4)]
     across = links.slot()
@@ -114,10 +115,14 @@
         ref = buf.at[place.ring(du, dv)]
         links.start(ref, ref, slot, device, batch)
 
+    def hand_over(du, dv):
+        chunk = place.ring(du, dv)
+        links.start(buf.at[chunk], kept.at[chunk], across, place.sibling(), batch)
+
     def spread(du):
         for way in (2, 1, 3):
             send(du, 0, far[du], place.at(0, way))
-        send(du, 0, across, place.sibling())
+        hand_over(du, 0)
 
     for way in (2, 1, 3):
         send(0, 0, near[way], place.at(way, 0))
@@ -130,9 +135,9 @@
     for du in (0, 3, 1, 2):
         links.wait(buf.at[pl.ds(0, 3)], far[du], place.at(0, 1))
         for way in (1, 3, 2):
-            send(du, way, across, place.sibling())
+            hand_over(du, way)
         yield
-    links.wait(buf.at[pl.ds(0, 16)], across, place.sibling())
+    links.wait(kept.at[pl.ds(0, 16)], across, place.sibling())
 
 
 def plane_sum(place, links, buf, sib, vland, uland):
@@ -393,7 +398,6 @@
     vland,
     uland,
     ycol,
-    yrow,
     gvalue,
     gsib,
     gchips,
@@ -572,18 +576,16 @@
     product = part[row] + swapped[col]
     ycol[row] = product
 
-    wide = plane_gather(place, links, ycol)
+    wide = plane_gather(place, links, ycol, ycol_out)
     next(wide)
-    turn = Turn(place, links, yrow, own, other)
+    turn = Turn(place, links, yrow_out, own, other)
     for step in range(8):
         piece = mod(col + step, 8)
         device = {"row": base + col, "col": piece}
-        turn.start(ycol.at[row], yrow.at[inner], device, None if step else other)
-
-    @pl.when(own)
-    def _():
-        yrow[inner] = product
-
+        turn.start(ycol.at[row], yrow_out.at[inner], device, None if step else other)
+
+    mine = pltpu.make_async_copy(ycol.at[row], yrow_out.at[inner], out_sem.at[10])
+    pl.when(own)(mine.start)
     next(nsum)
     inverse[...], _ = refine(scaled[...], inverse[...])
     for _ in range(3):
@@ -601,12 +603,6 @@
         copies.append(pltpu.make_async_copy(ref, out, out_sem.at[sem]))
         copies[-1].start()
 
-    def keep_cols(core, sem):
-        for chip in range(16):
-            chunk = 2 * chip + core
-            pltpu.make_async_copy(ycol.at[chunk], ycol_out.at[chunk], out_sem.at[sem]).start()
-        copies.append(pltpu.make_async_copy(ycol.at[pl.ds(0, 16)], ycol_out.at[pl.ds(0, 16)], out_sem.at[sem]))
-
     for _ in nsum:
         pass
     mix_hi[...], mix_lo[...] = mixing(inverse[...] * left * right, ntotal[...].reshape(K, K))
@@ -614,12 +610,14 @@
     for index, (ref, out) in enumerate(ends):
         keep(ref, out, 4 + index)
     next(wide)
-    keep_cols(place.core, 9)
+    for chip in range(16):
+        chunk = 2 * chip + place.core
+        pltpu.make_async_copy(ycol.at[chunk], ycol_out.at[chunk], out_sem.at[9]).start()
+    copies.append(pltpu.make_async_copy(ycol.at[pl.ds(0, 16)], ycol_out.at[pl.ds(0, 16)], out_sem.at[9]))
     turn.wait()
-    keep(yrow, yrow_out, 10)
+    pl.when(own)(mine.wait)
     for _ in wide:
         pass
-    keep_cols(1 - place.core, 11)
     for copy in copies:
         copy.wait()
     links.finish(place.sibling())
@@ -663,13 +661,10 @@
         pairs += [(ref.at[eight], land.at[eight]) for ref, land in ((ycol, yc), (acol_hi, ah), (acol_lo, al))]
         pairs.append((stored.at[:, k, :], s.at[k]))
     loads = [pltpu.make_async_copy(source, land, load_sem.at[index]) for index, (source, land) in enumerate(pairs)]
-    ahead = heads + 4
-    for load in loads[:ahead]:
+    for load in loads:
         load.start()
     for load in loads[:heads]:
         load.wait()
-    for load in loads[ahead : ahead + 4]:
-        load.start()
 
     @pl.when(jnp.max(size[...]) > 1e-6)
     def _():
@@ -697,12 +692,12 @@
     row_halves = [ref[...].reshape(TILE, K) for ref in (rh, rl)]
     wrow = split(dot3([jnp.concatenate(pair, 1) for pair in zip(yr_halves, row_halves)], mix))
     left_pair = [jnp.concatenate(pair, 1) for pair in zip(row_halves, wrow)]
-    stores = []
-    for k in range(SLOTS):
-        for load in loads[heads + 4 * k : heads + 4 * k + 4]:
-            load.wait()
-        for load in loads[ahead + 4 * k + 4 : ahead + 4 * k + 8]:
-            load.start()
+    stores = [pltpu.make_async_copy(s.at[k], out.at[:, k, :], out_sem.at[k]) for k in range(SLOTS)]
+
+    def tile(k, carry):
+        eight = pl.ds(8 * k, 8)
+        for index, ref in enumerate((yc.at[eight], ah.at[eight], al.at[eight], s.at[k])):
+            pltpu.make_async_copy(ref, ref, load_sem.at[heads + 4 * k + index]).wait()
 
         @pl.when(8 * k + col == row)
         def _():
@@ -717,14 +712,17 @@
 
         @pl.when(8 * k + col <= row)
         def _():
-            y_halves = split(yc[8 * k : 8 * k + 8].reshape(TILE, K))
-            a_halves = [ref[8 * k : 8 * k + 8].reshape(TILE, K) for ref in (ah, al)]
+            y_halves = split(yc[eight].reshape(TILE, K))
+            a_halves = [ref[eight].reshape(TILE, K) for ref in (ah, al)]
             wcol = split(dot3([jnp.concatenate(pair, 1) for pair in zip(y_halves, a_halves)], mix))
             right_pair = [jnp.concatenate(pair, 1) for pair in zip(wcol, a_halves)]
             s[k] -= dot3(left_pair, right_pair, NT)
 
-        stores.append(pltpu.make_async_copy(s.at[k], out.at[:, k, :], out_sem.at[k]))
-        stores[-1].start()
+        for index in range(SLOTS):
+            pl.when(k == index)(stores[index].start)
+        return carry
+
+    lax.fori_loop(0, SLOTS, tile, 0)
     for store in stores:
         store.wait()
 
@@ -769,7 +767,6 @@
             vmem((4, 3, CHUNK, K), F32),
             vmem((3, CHUNK, K), F32),
             vmem(col_shape, F32),
-            vmem(row_shape, F32),
             *small,
             *small,
             vmem((K, K), F32),
@@ -778,7 +775,7 @@
             vmem(wide, BF16),
             vmem((8, 128), F32),
             dma((SLOTS + 1,)),
-            dma((12,)),
+            dma((11,)),
             dma((SENDS,)),
             dma((RECVS,)),
         ],

time: 98.6 us -> 98.6 us (level)
    pallas_call x1, Pallas kernels: 22.5 us -> 23.7 us  [body(): pl.pallas_call(update_kernel, out_shape=jax.ShapeDtypeStruct(stored.shape...]
where the time goes in v4:
time: 98.6 us; the launch traced here: 98.5 us
  Pallas kernels  98.3 us (100%)
    pallas_call x1, Pallas kernels, body(): pl.pallas_call(exchange_kernel, out_shape=[jax.ShapeDtypeStruct(shape, ki...  74.6 us
    pallas_call x1, Pallas kernels, body(): pl.pallas_call(update_kernel, out_shape=jax.ShapeDtypeStruct(stored.shape...  23.7 us

profile of v4, /device:TPU:7, one launch (start us, length us, event | category | flops | bytes accessed | tf_op | source)
XLA Modules:
  0.0 98.5 jit_solution(11958641347541825571)
XLA Ops:
  0.0 74.6 %exchange.1 = (bf16[32,64,256]{2,1,0:T(8,128)(2,1)}, bf16[32,64,256]{2,1,0:T(8,128)(2,1)}, bf16[8,64,256]{2,1,0:T(8,128)(2,1)}, bf16[8,64,256]{2,1,0:T(8,128)(2,...) custom-call(f32[512,4,512]{2,1,0:T(4,128)} %stored.3, ...), custom_call_target="tpu_custom_call" | custom-call | tf_op jit(solution)/shard_map/exchange/pallas_call | solution.py:743
  74.6 23.7 %update.1 = f32[512,4,512]{2,1,0:T(4,128)} custom-call(f32[512,4,512]{2,1,0:T(4,128)} %stored.3, bf16[32,64,256]{2,1,0:T(8,128)(2,1)} %get-tuple-element.16.acol_hi, bf16[32,64,256]{2,1,0:T(8,128)(2,1)} %get-tuple-element.17.acol_lo, bf16[8,64,256]{2,1,0:T(8,128)(2,1)} %get-tuple-element.18.arow_hi, bf16[8,64,256]{2,1,0:T(8,128)(2,1)} %get-tuple-element.19.arow_lo, ...), custom_call_target="tpu_custom_call" | custom-call | tf_op jit(solution)/shard_map/update/pallas_call | solution.py:785

commit v5 on v4

--- a/solution.py
+++ b/solution.py
@@ -511,8 +511,9 @@
             part[8 * k : 8 * k + 8] = terms.reshape(8, CHUNK, K)
 
         next(tall)
-        if k < 3:
+        if k < 2:
             next(wide)
+    next(wide)
     next(tall)
     next(gsum)
     for _ in wide:

time: 98.6 us -> 98.5 us (level)
  no operation moved by 1% of the time
where the time goes in v5:
time: 98.5 us; the launch traced here: 98.4 us
  Pallas kernels  98.2 us (100%)
    pallas_call x1, Pallas kernels, body(): pl.pallas_call(exchange_kernel, out_shape=[jax.ShapeDtypeStruct(shape, ki...  74.5 us
    pallas_call x1, Pallas kernels, body(): pl.pallas_call(update_kernel, out_shape=jax.ShapeDtypeStruct(stored.shape...  23.7 us

profile of v5, /device:TPU:7, one launch (start us, length us, event | category | flops | bytes accessed | tf_op | source)
XLA Modules:
  0.0 98.4 jit_solution(9318480299241484240)
XLA Ops:
  0.0 74.5 %exchange.1 = (bf16[32,64,256]{2,1,0:T(8,128)(2,1)}, bf16[32,64,256]{2,1,0:T(8,128)(2,1)}, bf16[8,64,256]{2,1,0:T(8,128)(2,1)}, bf16[8,64,256]{2,1,0:T(8,128)(2,...) custom-call(f32[512,4,512]{2,1,0:T(4,128)} %stored.3, ...), custom_call_target="tpu_custom_call" | custom-call | tf_op jit(solution)/shard_map/exchange/pallas_call | solution.py:744
  74.5 23.7 %update.1 = f32[512,4,512]{2,1,0:T(4,128)} custom-call(f32[512,4,512]{2,1,0:T(4,128)} %stored.3, bf16[32,64,256]{2,1,0:T(8,128)(2,1)} %get-tuple-element.16.acol_hi, bf16[32,64,256]{2,1,0:T(8,128)(2,1)} %get-tuple-element.17.acol_lo, bf16[8,64,256]{2,1,0:T(8,128)(2,1)} %get-tuple-element.18.arow_hi, bf16[8,64,256]{2,1,0:T(8,128)(2,1)} %get-tuple-element.19.arow_lo, ...), custom_call_target="tpu_custom_call" | custom-call | tf_op jit(solution)/shard_map/update/pallas_call | solution.py:786
